TPU v7x, 32 devices: a whole 2x2x4 slice. The times are simulated.
32 devices in a mesh: img: 8 (over z, x), lat: 4 (over y, core).
Axes of the slice: x: 2, y: 2, z: 4, core: 2. Of those that a mesh axis runs over, the one named last changes fastest.
Arguments:
- media: bfloat16 [98304, 1024], P(('img', 'lat')), may hold values from -6 to 6
- latents: float32 [192, 64, 1024], P('img', 'lat'), may hold values from -6 to 6
- counts: int32 [8, 24], P('img'), may hold values from 1 to 6, 48 in all within a row
- cotangent: bfloat16 [192, 64, 1024], P('img', 'lat'), may hold values from -6 to 6
- attend_weight: float32 [1024, 1536], P(('img', 'lat')), may hold values from -0.1875 to 0.1875
- output_weight: float32 [512, 1024], P(('img', 'lat')), may hold values from -4 to 4
- expand_weight: float32 [1024, 4096], P(('img', 'lat')), may hold values from -0.1875 to 0.1875
- shrink_weight: float32 [4096, 1024], P(('img', 'lat')), may hold values from -0.09375 to 0.09375
- layer_gains: float32 [1024, 3], P(('img', 'lat')), may hold values from 0.24 to 3.6
- layer_biases: float32 [1024, 3], P(('img', 'lat')), may hold values from -1.2 to 1.2
- attend_momentum: float32 [1024, 1536], P(('img', 'lat')), may hold values from -0.00021362305 to 0.00021362305
- output_momentum: float32 [512, 1024], P(('img', 'lat')), may hold values from -0.00021362305 to 0.00021362305
- expand_momentum: float32 [1024, 4096], P(('img', 'lat')), may hold values from -0.00021362305 to 0.00021362305
- shrink_momentum: float32 [4096, 1024], P(('img', 'lat')), may hold values from -0.00021362305 to 0.00021362305
- gains_momentum: float32 [1024, 3], P(('img', 'lat')), may hold values from -0.0008544922 to 0.0008544922
- biases_momentum: float32 [1024, 3], P(('img', 'lat')), may hold values from -0.0008544922 to 0.0008544922
- attend_average: float32 [1024, 1536], P(('img', 'lat')), may hold values from -0.1875 to 0.1875
- output_average: float32 [512, 1024], P(('img', 'lat')), may hold values from -4 to 4
- expand_average: float32 [1024, 4096], P(('img', 'lat')), may hold values from -0.1875 to 0.1875
- shrink_average: float32 [4096, 1024], P(('img', 'lat')), may hold values from -0.09375 to 0.09375
- gains_average: float32 [1024, 3], P(('img', 'lat')), may hold values from 0.5 to 1.5
- biases_average: float32 [1024, 3], P(('img', 'lat')), may hold values from -1.2 to 1.2
Outputs:
- latents_out: float32 [192, 64, 1024], P('img', 'lat')
- media_grad: bfloat16 [98304, 1024], P(('img', 'lat'))
- latents_grad: float32 [192, 64, 1024], P('img', 'lat')
- grad_norm: float32 [], replicated
- attend_master: float32 [1024, 1536], P(('img', 'lat'))
- output_master: float32 [512, 1024], P(('img', 'lat'))
- expand_master: float32 [1024, 4096], P(('img', 'lat'))
- shrink_master: float32 [4096, 1024], P(('img', 'lat'))
- gains_master: float32 [1024, 3], P(('img', 'lat'))
- biases_master: float32 [1024, 3], P(('img', 'lat'))
- attend_buffer: float32 [1024, 1536], P(('img', 'lat'))
- output_buffer: float32 [512, 1024], P(('img', 'lat'))
- expand_buffer: float32 [1024, 4096], P(('img', 'lat'))
- shrink_buffer: float32 [4096, 1024], P(('img', 'lat'))
- gains_buffer: float32 [1024, 3], P(('img', 'lat'))
- biases_buffer: float32 [1024, 3], P(('img', 'lat'))
- attend_smoothed: float32 [1024, 1536], P(('img', 'lat'))
- output_smoothed: float32 [512, 1024], P(('img', 'lat'))
- expand_smoothed: float32 [1024, 4096], P(('img', 'lat'))
- shrink_smoothed: float32 [4096, 1024], P(('img', 'lat'))
- gains_smoothed: float32 [1024, 3], P(('img', 'lat'))
- biases_smoothed: float32 [1024, 3], P(('img', 'lat'))
Inputs may be any that keep to these rules, and one draw needn't show every extreme that they name: Each row of counts holds 24 whole numbers that sum to 48; the largest of a row is exactly 6.
All inputs are finite; a program needn't handle non-finite values.
Results may differ from a plain program's by a relative error of at most 0.017.
The roundings to bfloat16 on the way count: a program that leaves them out, or rounds other values in their place, can miss the bound.
Values may be sent and summed in bfloat16 or wider, within the bound.
A program may use at most 256 MiB of HBM per device.

v0:
```python
import math

import jax
import jax.numpy as jnp
from jax import lax
from jax.sharding import PartitionSpec as P

D = 1024
HEADS = 8
HDIM = 64
FF = 4096
PATCH_IMG = 256
INNER = 512


EPS = 1e-05
MOMENTUM = 0.9
DECAY = 0.0001
AVERAGING = 0.6
CLIP_NORM = 1.0
MASKED = -1e30
PAIRED = 2
RATE_SCALES = (1.0, 100.0, 1.0, 1.0, 15.0, 1.0)


def merged(value, axis, join):
    pieces = jax.tree.map(lambda part: lax.all_gather(part, axis), value)
    head = jax.tree.map(lambda part: part[0], pieces)
    tail = jax.tree.map(lambda part: part[1:], pieces)
    total, _ = lax.scan(lambda total, section: (join(total, section), None), head, tail)
    return total


def to_half(values):
    return values.astype(jnp.bfloat16)


def matmul(first_op, second_op):
    return jnp.dot(first_op, second_op, preferred_element_type=jnp.float32)


def matmul_left_t(first_op, second_op):
    return lax.dot_general(
        first_op, second_op, (((0,), (0,)), ((), ())), preferred_element_type=jnp.float32
    )


def matmul_right_t(first_op, second_op):
    return lax.dot_general(
        first_op, second_op, (((1,), (1,)), ((), ())), preferred_element_type=jnp.float32
    )


def layer_norm(values, norm_gain, norm_bias):
    center = values - jnp.mean(values, axis=-1, keepdims=True)
    spread = jnp.mean(center * center, axis=-1, keepdims=True)
    return center * lax.rsqrt(spread + EPS) * norm_gain + norm_bias


def gelu_exact(values):
    return jax.nn.gelu(values, approximate=False)


def step_size():
    return 0.37 * math.sqrt((4 * D * INNER + 2 * D * FF) / D)


def combine_stats(first_pair, second_pair):
    top_both = jnp.maximum(first_pair[0], second_pair[0])
    total_both = first_pair[1] * jnp.exp(first_pair[0] - top_both) + second_pair[1] * jnp.exp(
        second_pair[0] - top_both
    )
    return (top_both, total_both)


def shards(
    media,
    latents,
    counts,
    cotangent,
    attend_weight,
    output_weight,
    expand_weight,
    shrink_weight,
    layer_gains,
    layer_biases,
    attend_momentum,
    output_momentum,
    expand_momentum,
    shrink_momentum,
    gains_momentum,
    biases_momentum,
    attend_average,
    output_average,
    expand_average,
    shrink_average,
    gains_average,
    biases_average,
):
    w_attend, w_output, w_expand, w_shrink, gain_rows, bias_rows = (
        lax.all_gather(to_half(attend_weight), ("img", "lat"), axis=0, tiled=True),
        lax.all_gather(to_half(output_weight), ("img", "lat"), axis=0, tiled=True),
        lax.all_gather(to_half(expand_weight), ("img", "lat"), axis=0, tiled=True),
        lax.all_gather(to_half(shrink_weight), ("img", "lat"), axis=0, tiled=True),
        lax.all_gather(to_half(layer_gains), ("img", "lat"), axis=0, tiled=True),
        lax.all_gather(to_half(layer_biases), ("img", "lat"), axis=0, tiled=True),
    )
    gain_all = gain_rows.astype(jnp.float32)
    bias_all = bias_rows.astype(jnp.float32)
    lat_count = lax.axis_size("lat")
    samples, lat_dev, model_width = latents.shape
    inner = HEADS * HDIM
    patch_dev = media.shape[0]
    group_patches = patch_dev * lat_count
    row_count = samples * lat_dev
    head_count = HEADS
    score_scale = HDIM ** (-0.5)
    sample_ends = jnp.cumsum(counts[0])
    image_ids = jnp.sum(
        (
            jnp.arange(group_patches // PATCH_IMG, dtype=jnp.int32)[:, None] >= sample_ends[None, :]
        ).astype(jnp.int32),
        axis=1,
    )

    def make_view(queries, image_list, key_ids, key_rows, value_rows, width):
        block_keys = width * PATCH_IMG

        def view(block_index):
            first_key = block_index * block_keys
            low_sample = jnp.clip(image_list[block_index * width], 0, samples - width)
            window_query = lax.dynamic_slice_in_dim(queries, low_sample, width, 0)
            window_ids = low_sample + jnp.arange(width, dtype=jnp.int32)
            block_ids = lax.dynamic_slice_in_dim(key_ids, first_key, block_keys, 0)
            key_block = lax.dynamic_slice_in_dim(key_rows, first_key, block_keys, 0)
            value_block = lax.dynamic_slice_in_dim(value_rows, first_key, block_keys, 0)
            allowed = window_ids[:, None] == block_ids[None, :]
            scores = (
                jnp.einsum(
                    "sqhd,khd->shqk", window_query, key_block, preferred_element_type=jnp.float32
                )
                * score_scale
            )
            scores = jnp.where(allowed[:, None, None, :], scores, MASKED)
            return (first_key, low_sample, window_query, key_block, value_block, scores)

        return view

    media_float = media.astype(jnp.float32)
    normed_media_f, media_back = jax.vjp(layer_norm, media_float, gain_all[:, 0], bias_all[:, 0])
    normed_media = to_half(normed_media_f)
    latent_flat = latents.reshape(row_count, model_width)
    normed_latent_f, latent_back = jax.vjp(layer_norm, latent_flat, gain_all[:, 1], bias_all[:, 1])
    latent_rows = to_half(normed_latent_f)
    query_rows = to_half(matmul(latent_rows, w_attend[:, :inner]))
    latent_major = jnp.transpose(
        latent_rows.reshape(samples, lat_dev, model_width), (1, 0, 2)
    ).reshape(row_count, model_width)
    own_rows = jnp.concatenate([normed_media, latent_major], axis=0)
    kv_weight = w_attend[:, inner:]
    projected = matmul(own_rows, kv_weight)
    key_own = to_half(projected[:, :inner])
    value_own = to_half(projected[:, inner:])
    key_patch = key_own[:patch_dev].reshape(patch_dev, head_count, HDIM)
    value_patch = value_own[:patch_dev].reshape(patch_dev, head_count, HDIM)
    key_latent = jnp.transpose(
        key_own[patch_dev:].reshape(lat_dev, samples, head_count, HDIM), (1, 0, 2, 3)
    )
    value_latent = jnp.transpose(
        value_own[patch_dev:].reshape(lat_dev, samples, head_count, HDIM), (1, 0, 2, 3)
    )
    query_all = lax.all_gather(
        query_rows.reshape(samples, lat_dev, inner), "lat", axis=1, tiled=True
    ).reshape(samples, lat_dev * lat_count, head_count, HDIM)
    local_images = patch_dev // PATCH_IMG
    local_ids = lax.dynamic_slice_in_dim(
        image_ids, lax.axis_index("lat") * local_images, local_images, 0
    )
    local_patch_ids = jnp.repeat(local_ids, PATCH_IMG)
    local_blocks = local_images // PAIRED
    view = make_view(query_all, local_ids, local_patch_ids, key_patch, value_patch, PAIRED)
    latent_scores = (
        jnp.einsum("sqhd,skhd->shqk", query_all, key_latent, preferred_element_type=jnp.float32)
        * score_scale
    )
    row_top = jnp.max(latent_scores, axis=-1)
    row_total = jnp.sum(jnp.exp(latent_scores - row_top[..., None]), axis=-1)

    def stats_step(block_index, loop_state):
        top_all, total_all = loop_state
        first_key, low_sample, window_query, key_block, value_block, scores = view(block_index)
        old_top = lax.dynamic_slice_in_dim(top_all, low_sample, PAIRED, 0)
        old_total = lax.dynamic_slice_in_dim(total_all, low_sample, PAIRED, 0)
        new_top = jnp.maximum(old_top, jnp.max(scores, axis=-1))
        new_total = old_total * jnp.exp(old_top - new_top) + jnp.sum(
            jnp.exp(scores - new_top[..., None]), axis=-1
        )
        return (
            lax.dynamic_update_slice_in_dim(top_all, new_top, low_sample, 0),
            lax.dynamic_update_slice_in_dim(total_all, new_total, low_sample, 0),
        )

    row_top, row_total = lax.fori_loop(0, local_blocks, stats_step, (row_top, row_total))
    row_top, row_total = merged((row_top, row_total), "lat", combine_stats)
    log_total = row_top + jnp.log(row_total)
    latent_probs = jnp.exp(latent_scores - log_total[..., None])
    latent_probs_half = to_half(latent_probs)
    context_part = jnp.einsum(
        "shqk,skhd->sqhd", latent_probs_half, value_latent, preferred_element_type=jnp.float32
    )

    def context_step(block_index, context_now):
        first_key, low_sample, window_query, key_block, value_block, scores = view(block_index)
        window_lse = lax.dynamic_slice_in_dim(log_total, low_sample, PAIRED, 0)
        block_probs = to_half(jnp.exp(scores - window_lse[..., None]))
        block_part = jnp.einsum(
            "shqk,khd->sqhd", block_probs, value_block, preferred_element_type=jnp.float32
        )
        old_part = lax.dynamic_slice_in_dim(context_now, low_sample, PAIRED, 0)
        return lax.dynamic_update_slice_in_dim(context_now, old_part + block_part, low_sample, 0)

    context_part = lax.fori_loop(0, local_blocks, context_step, context_part)
    context = (
        lax.psum_scatter(
            context_part.reshape(samples, lat_dev * lat_count, inner).astype(jnp.bfloat16),
            "lat",
            scatter_dimension=1,
            tiled=True,
        )
        .astype(jnp.float32)
        .reshape(samples, lat_dev, head_count, HDIM)
    )
    context_half = to_half(context.reshape(row_count, inner))
    mixed_rows = latent_flat + matmul(context_half, w_output)
    normed_mixed_f, mixed_back = jax.vjp(layer_norm, mixed_rows, gain_all[:, 2], bias_all[:, 2])
    normed_half = to_half(normed_mixed_f)
    pre_act = matmul(normed_half, w_expand)
    activated, act_back = jax.vjp(gelu_exact, pre_act)
    hidden_half = to_half(activated)
    result_rows = mixed_rows + matmul(hidden_half, w_shrink)
    grad_out = cotangent.astype(jnp.float32).reshape(row_count, model_width)
    grad_out_half = to_half(grad_out)
    grad_shrink = matmul_left_t(hidden_half, grad_out_half)
    grad_hidden = matmul_right_t(grad_out_half, w_shrink)
    grad_pre = to_half(act_back(grad_hidden)[0])
    grad_expand = matmul_left_t(normed_half, grad_pre)
    grad_normed = matmul_right_t(grad_pre, w_expand)
    grad_mixed_ln, grad_gain_ff, grad_bias_ff = mixed_back(grad_normed)
    grad_mixed = grad_out + grad_mixed_ln
    grad_attended = to_half(grad_mixed)
    grad_output = matmul_left_t(context_half, grad_attended)
    grad_context = to_half(matmul_right_t(grad_attended, w_output)).reshape(
        samples, lat_dev, head_count, HDIM
    )
    own_delta = jnp.einsum("sqhd,sqhd->sqh", grad_context.astype(jnp.float32), context)
    grad_all, delta_all = (
        lax.all_gather(
            grad_context.astype(jnp.float32).astype(jnp.bfloat16), "lat", axis=1, tiled=True
        ).astype(jnp.float32),
        lax.all_gather(own_delta.astype(jnp.bfloat16), "lat", axis=1, tiled=True).astype(
            own_delta.dtype
        ),
    )
    grad_all = to_half(grad_all)
    delta_all = jnp.transpose(delta_all, (0, 2, 1))
    grad_prob = jnp.einsum(
        "sqhd,skhd->shqk", grad_all, value_latent, preferred_element_type=jnp.float32
    )
    dscore = to_half(latent_probs * (grad_prob - delta_all[..., None]))
    query_part = score_scale * jnp.einsum(
        "shqk,skhd->sqhd", dscore, key_latent, preferred_element_type=jnp.float32
    )
    grad_key_latent = score_scale * jnp.einsum(
        "shqk,sqhd->skhd", dscore, query_all, preferred_element_type=jnp.float32
    )
    grad_value_latent = jnp.einsum(
        "shqk,sqhd->skhd", latent_probs_half, grad_all, preferred_element_type=jnp.float32
    )
    delta = delta_all
    grad_ctx = grad_all
    start_query = query_part

    def grad_step(block_index, loop_state):
        grad_query_now, grad_key_patch, grad_value_patch = loop_state
        first_key, low_sample, window_query, key_block, value_block, scores = view(block_index)
        window_lse = lax.dynamic_slice_in_dim(log_total, low_sample, PAIRED, 0)
        window_delta = lax.dynamic_slice_in_dim(delta, low_sample, PAIRED, 0)
        window_grad = lax.dynamic_slice_in_dim(grad_ctx, low_sample, PAIRED, 0)
        block_probs = jnp.exp(scores - window_lse[..., None])
        block_grad_prob = jnp.einsum(
            "sqhd,khd->shqk", window_grad, value_block, preferred_element_type=jnp.float32
        )
        block_dscore = to_half(block_probs * (block_grad_prob - window_delta[..., None]))
        query_part = score_scale * jnp.einsum(
            "shqk,khd->sqhd", block_dscore, key_block, preferred_element_type=jnp.float32
        )
        key_part = score_scale * jnp.einsum(
            "shqk,sqhd->khd", block_dscore, window_query, preferred_element_type=jnp.float32
        )
        value_part = jnp.einsum(
            "shqk,sqhd->khd", to_half(block_probs), window_grad, preferred_element_type=jnp.float32
        )
        old_query = lax.dynamic_slice_in_dim(grad_query_now, low_sample, PAIRED, 0)
        grad_query_now = lax.dynamic_update_slice_in_dim(
            grad_query_now, old_query + query_part, low_sample, 0
        )
        grad_key_patch = lax.dynamic_update_slice_in_dim(grad_key_patch, key_part, first_key, 0)
        grad_value_patch = lax.dynamic_update_slice_in_dim(
            grad_value_patch, value_part, first_key, 0
        )
        return (grad_query_now, grad_key_patch, grad_value_patch)

    empty_patch = jnp.zeros((patch_dev, head_count, HDIM), jnp.float32)
    query_part, grad_key_patch, grad_value_patch = lax.fori_loop(
        0, local_blocks, grad_step, (start_query, empty_patch, empty_patch)
    )
    grad_query = lax.psum_scatter(
        query_part.reshape(samples, lat_dev * lat_count, inner).astype(jnp.bfloat16),
        "lat",
        scatter_dimension=1,
        tiled=True,
    ).astype(jnp.float32)
    key_grads = jnp.concatenate(
        [
            grad_key_patch.reshape(patch_dev, inner),
            jnp.transpose(grad_key_latent, (1, 0, 2, 3)).reshape(row_count, inner),
        ],
        axis=0,
    )
    value_grads = jnp.concatenate(
        [
            grad_value_patch.reshape(patch_dev, inner),
            jnp.transpose(grad_value_latent, (1, 0, 2, 3)).reshape(row_count, inner),
        ],
        axis=0,
    )
    grad_kv_half = to_half(jnp.concatenate([key_grads, value_grads], axis=1))
    grad_kv_weight = matmul_left_t(own_rows, grad_kv_half)
    grad_rows = matmul_right_t(grad_kv_half, kv_weight)
    grad_query_half = to_half(grad_query.reshape(row_count, inner))
    grad_query_weight = matmul_left_t(latent_rows, grad_query_half)
    latent_from_kv = (
        grad_rows[patch_dev:]
        .reshape(lat_dev, samples, model_width)
        .transpose(1, 0, 2)
        .reshape(row_count, model_width)
    )
    grad_latent_normed = matmul_right_t(grad_query_half, w_attend[:, :inner]) + latent_from_kv
    grad_media, grad_gain_media, grad_bias_media = media_back(grad_rows[:patch_dev])
    grad_latent_ln, grad_gain_latent, grad_bias_latent = latent_back(grad_latent_normed)
    latents_grad = (grad_mixed + grad_latent_ln).reshape(samples, lat_dev, model_width)
    grad_attend = jnp.concatenate([grad_query_weight, grad_kv_weight], axis=1)
    grad_gains = jnp.stack([grad_gain_media, grad_gain_latent, grad_gain_ff], axis=1)
    grad_biases = jnp.stack([grad_bias_media, grad_bias_latent, grad_bias_ff], axis=1)
    owned_grads = (
        lax.psum_scatter(grad_attend, ("img", "lat"), scatter_dimension=0, tiled=True),
        lax.psum_scatter(grad_output, ("img", "lat"), scatter_dimension=0, tiled=True),
        lax.psum_scatter(grad_expand, ("img", "lat"), scatter_dimension=0, tiled=True),
        lax.psum_scatter(grad_shrink, ("img", "lat"), scatter_dimension=0, tiled=True),
        lax.psum_scatter(grad_gains, ("img", "lat"), scatter_dimension=0, tiled=True),
        lax.psum_scatter(grad_biases, ("img", "lat"), scatter_dimension=0, tiled=True),
    )
    squares = sum((jnp.sum(piece * piece) for piece in owned_grads))
    grad_norm = jnp.sqrt(lax.psum(squares, ("img", "lat")))
    factor = jnp.minimum(1.0, CLIP_NORM / (grad_norm + 1e-06))
    masters = (
        attend_weight,
        output_weight,
        expand_weight,
        shrink_weight,
        layer_gains,
        layer_biases,
    )
    moments = (
        attend_momentum,
        output_momentum,
        expand_momentum,
        shrink_momentum,
        gains_momentum,
        biases_momentum,
    )
    averages = (
        attend_average,
        output_average,
        expand_average,
        shrink_average,
        gains_average,
        biases_average,
    )
    decay_rates = (DECAY, DECAY, DECAY, DECAY, 0.0, 0.0)
    step_rate = step_size()
    new_masters = []
    new_buffers = []
    new_smoothed = []
    for master, moment, average, reduced, decay_rate, rate_scale in zip(
        masters, moments, averages, owned_grads, decay_rates, RATE_SCALES
    ):
        step_grad = factor * reduced + decay_rate * master
        buffer = MOMENTUM * moment + step_grad
        master_new = master - step_rate * rate_scale * (step_grad + MOMENTUM * buffer)
        new_masters.append(master_new)
        new_buffers.append(buffer)
        new_smoothed.append(AVERAGING * average + (1.0 - AVERAGING) * master_new)
    latents_out = result_rows.reshape(samples, lat_dev, model_width)
    media_grad = grad_media.astype(jnp.bfloat16)
    return (
        latents_out,
        media_grad,
        latents_grad,
        grad_norm,
        new_masters[0],
        new_masters[1],
        new_masters[2],
        new_masters[3],
        new_masters[4],
        new_masters[5],
        new_buffers[0],
        new_buffers[1],
        new_buffers[2],
        new_buffers[3],
        new_buffers[4],
        new_buffers[5],
        new_smoothed[0],
        new_smoothed[1],
        new_smoothed[2],
        new_smoothed[3],
        new_smoothed[4],
        new_smoothed[5],
    )


def solution(mesh):
    return jax.shard_map(
        shards,
        mesh=mesh,
        in_specs=(
            P(("img", "lat"), None),
            P("img", "lat", None),
            P("img", None),
            P("img", "lat", None),
            P(("img", "lat"), None),
            P(("img", "lat"), None),
            P(("img", "lat"), None),
            P(("img", "lat"), None),
            P(("img", "lat"), None),
            P(("img", "lat"), None),
            P(("img", "lat"), None),
            P(("img", "lat"), None),
            P(("img", "lat"), None),
            P(("img", "lat"), None),
            P(("img", "lat"), None),
            P(("img", "lat"), None),
            P(("img", "lat"), None),
            P(("img", "lat"), None),
            P(("img", "lat"), None),
            P(("img", "lat"), None),
            P(("img", "lat"), None),
            P(("img", "lat"), None),
        ),
        out_specs=(
            P("img", "lat", None),
            P(("img", "lat"), None),
            P("img", "lat", None),
            P(),
            P(("img", "lat"), None),
            P(("img", "lat"), None),
            P(("img", "lat"), None),
            P(("img", "lat"), None),
            P(("img", "lat"), None),
            P(("img", "lat"), None),
            P(("img", "lat"), None),
            P(("img", "lat"), None),
            P(("img", "lat"), None),
            P(("img", "lat"), None),
            P(("img", "lat"), None),
            P(("img", "lat"), None),
            P(("img", "lat"), None),
            P(("img", "lat"), None),
            P(("img", "lat"), None),
            P(("img", "lat"), None),
            P(("img", "lat"), None),
            P(("img", "lat"), None),
        ),
        check_vma=False,
    )
```

profile of v0, /device:TPU:0, one launch (start us, length us, event | category | flops | bytes accessed | tf_op | source)
XLA Modules:
  0.0 1605.7 jit_solution(13362291207761276639)
XLA Ops:
  9.7 43.3 %all-gather.3 = bf16[32,32,3]{1,2,0:T(4,128)(2,1)S(1)} all-gather(bf16[1,32,3]{1,2,0:T(4,128)(2,1)S(1)} %convert_bitcast_fusion.1), channel_id=1, replica_groups=mesh['img'=8,'lat'=4] {'img','lat'}, dimensions={0}, use_global_device_ids=true | all-gather | bytes 6336 | tf_op jit(solution)/shard_map/all_gather | solution.py:106
  53.8 36.7 %all-gather.2 = bf16[32,32,3]{1,2,0:T(4,128)(2,1)S(1)} all-gather(bf16[1,32,3]{1,2,0:T(4,128)(2,1)S(1)} %convert_bitcast_fusion.2), channel_id=1, replica_groups=mesh['img'=8,'lat'=4] {'img','lat'}, dimensions={0}, use_global_device_ids=true | all-gather | bytes 6336 | tf_op jit(solution)/shard_map/all_gather | solution.py:105
  115.5 11.5 convolution_convert_fusion
  151.5 35.0 %while.57 = (s32[]{:T(128)}, f32[24,8,64]{2,1,0:T(8,128)S(1)}, f32[24,8,64]{2,1,0:T(8,128)}, s32[12]{0:T(128)S(1)}, s32[3072]{0:T(1024)}, /*index=5*/bf16[3072,8...) while((s32[]{:T(128)}, f32[24,8,64]{2,1,0:T(8,128)S(1)}, ...), condition=%wide.region_11.12_spmd, body=%wide.region_8.11_spmd.sunk | while | flops 70782984 | bytes 7444285 | solution.py:203
  211.2 37.9 %while.59 = (s32[]{:T(128)}, f32[24,64,8,64]{1,3,0,2:T(8,128)}, s32[12]{0:T(128)S(1)}, bf16[3072,8,64]{0,2,1:T(8,128)(2,1)}, s32[3072]{0:T(1024)}, /*index=5*/bf...) while((s32[]{:T(128)}, f32[24,64,8,64]{1,3,0,2:T(8,128)}, ...), condition=%wide.region_15.16_spmd, body=%wide.region_14.15_spmd.sunk | while | flops 136381440 | bytes 6837061 | solution.py:222
  267.7 24.0 %reduce-scatter.15.cloned.1.call-done = bf16[24,16,512]{2,1,0:T(8,128)(2,1)} async-done(((bf16[24,64,512]{2,1,0:T(8,128)(2,1)}), bf16[24,16,512]{2,1,0:T(8,128)(2,1)}) %reduce-scatter.15.cloned.1.call-update) | async-done | bytes 393232 | tf_op jit(solution)/shard_map/reduce_scatter | solution.py:224
  294.1 78.9 %all-gather.17.cloned.1.call-done = bf16[1024,4096]{1,0:T(8,128)(2,1)} async-done(((bf16[32,4096]{1,0:T(8,128)(2,1)}), bf16[1024,4096]{1,0:T(8,128)(2,1)}) %all-gather.17.cloned.1.call-update) | async-done | bytes 8388624 | tf_op jit(solution)/shard_map/all_gather | solution.py:103
  373.0 9.3 fusion.109
  382.3 70.6 %all-gather.19.cloned.1.call-done = bf16[4096,1024]{1,0:T(8,128)(2,1)} async-done(((bf16[128,1024]{1,0:T(8,128)(2,1)}), bf16[4096,1024]{1,0:T(8,128)(2,1)}) %all-gather.19.cloned.1.call-update) | async-done | bytes 8388624 | tf_op jit(solution)/shard_map/all_gather | solution.py:104
  452.9 20.7 %add_convert_fusion.1 = (bf16[384,4096]{1,0:T(8,128)(2,1)S(1)}, f32[384,4096]{1,0:T(8,128)}) fusion(f32[384,4096]{1,0:T(8,128)} %fusion.109, bf16[384,1024]{1,0:T(8,128)(2,1)S(1)} %bitcast.302, bf16[4096,1024]{1,0:T(8,128)(2,1)} %all-gather.19.cloned.1.call-done), kind=kOutput, calls=%fused_computation.104 | convolution fusion | flops 3334471680 | bytes 24903680 | tf_op jit(solution)/shard_map/dot_general | solution.py:49
  495.4 15.6 all-gather.21.cloned.1.call-done
  524.0 83.2 %while.60 = (s32[]{:T(128)}, f32[24,64,8,64]{1,3,0,2:T(8,128)}, bf16[3072,8,64]{0,2,1:T(8,128)(2,1)}, bf16[3072,8,64]{0,2,1:T(8,128)(2,1)}, s32[12]{0:T(128)S(1)...) while((s32[]{:T(128)}, f32[24,64,8,64]{1,3,0,2:T(8,128)}, ...), condition=%wide.region_22.23_spmd, body=%wide.region_21.22_spmd.sunk | while | flops 341181440 | bytes 19699572 | solution.py:314
  628.7 25.3 %fusion.74 = f32[3456,1024]{1,0:T(8,128)} fusion(bf16[1024,1536]{1,0:T(8,128)(2,1)} %all-gather.11.cloned.1.call-done, bf16[384,512]{0,1:T(8,128)(2,1)S(1)} %copy.232, bf16[3072,512]{0,1:T(8,128)(2,1)} %bitcast.308, bf16[384,512]{0,1:T(8,128)(2,1)S(1)} %copy.230, bf16[3072,512]{0,1:T(8,128)(2,1)} %bitcast.306), kind=kOutput, calls=%fused_computation.127 | convolution fusion | flops 7276068864 | bytes 23330816 | tf_op jit(solution)/shard_map/dot_general | solution.py:49
  664.9 14.5 fusion.69
  702.0 10.2 fusion.108
  728.5 9.4 convolution_add_fusion
  738.0 11.8 fusion.111
  758.0 28.0 %reduce-scatter.19.cloned.1.call-done = f32[16,1024]{1,0:T(8,128)} async-done(((f32[512,1024]{1,0:T(8,128)}), f32[16,1024]{1,0:T(8,128)}) %reduce-scatter.19.cloned.1.call-update) | async-done | bytes 65552 | tf_op jit(solution)/shard_map/reduce_scatter | solution.py:357
  790.8 127.8 %reduce-scatter.27.cloned.1.call-done = f32[32,3]{1,0:T(8,128)} async-done(((f32[1024,3]{1,0:T(8,128)}), f32[32,3]{1,0:T(8,128)}) %reduce-scatter.27.cloned.1.call-update) | async-done | bytes 400
  919.4 132.0 %reduce-scatter.29.cloned.1.call-done = f32[32,3]{1,0:T(8,128)} async-done(((f32[1024,3]{1,0:T(8,128)}), f32[32,3]{1,0:T(8,128)}) %reduce-scatter.29.cloned.1.call-update) | async-done | bytes 400
  1053.4 115.0 %reduce-scatter.25.cloned.1.call-done = f32[32,1536]{1,0:T(8,128)} async-done(((f32[1024,1536]{1,0:T(8,128)}), f32[32,1536]{1,0:T(8,128)}) %reduce-scatter.25.cloned.1.call-update) | async-done | bytes 196624 | tf_op jit(solution)/shard_map/reduce_scatter | solution.py:356
  1171.7 181.2 %reduce-scatter.21.cloned.1.call-done = f32[32,4096]{1,0:T(8,128)} async-done(((f32[1024,4096]{1,0:T(8,128)}), f32[32,4096]{1,0:T(8,128)}) %reduce-scatter.21.cloned.1.call-update) | async-done | bytes 524304 | tf_op jit(solution)/shard_map/reduce_scatter | solution.py:358
  1355.4 184.3 %reduce-scatter.23.cloned.1.call-done = f32[128,1024]{1,0:T(8,128)} async-done(((f32[4096,1024]{1,0:T(8,128)}), f32[128,1024]{1,0:T(8,128)}) %reduce-scatter.23.cloned.1.call-update) | async-done | bytes 524304 | tf_op jit(solution)/shard_map/reduce_scatter | solution.py:359
  1546.4 41.7 %psum.7 = f32[]{:T(128)} all-reduce(f32[]{:T(128)S(6)} %add.422), channel_id=1, replica_groups=mesh['img'=8,'lat'=4] {'img','lat'}, use_global_device_ids=true, to_apply=%region_46.47 | all-reduce | flops 1 | bytes 8 | tf_op jit(solution)/shard_map/psum | solution.py:364
  (552 shorter events, 383.1 us)
Async XLA Ops:
  7.2 85.1 %copy-start = (f32[24,16,1024]{2,1,0:T(8,128)S(1)}, f32[24,16,1024]{2,1,0:T(8,128)}, u32[]{:S(2)}) copy-start(f32[24,16,1024]{2,1,0:T(8,128)} %param.31) | copy-start | bytes 4718596
  7.2 86.7 %all-gather.11.cloned.1.call-start = ((), (), s32[]{:S(2)}) async-start(), calls=%async_computation.8 | async-start | bytes 3244032 | tf_op jit(solution)/shard_map/all_gather | solution.py:101
  9.0 128.8 %all-gather.13.cloned.1.call-start = ((), (), s32[]{:S(2)}) async-start(), calls=%async_computation.9 | async-start | bytes 1966080 | tf_op jit(solution)/shard_map/all_gather | solution.py:172
  93.3 279.7 %copy-start.45 = (f32[1024,1]{0,1:T(1,128)}, f32[1024,1]{0,1:T(1,128)S(1)}, u32[]{:S(2)}) copy-start(f32[1024,1]{0,1:T(1,128)S(1)} %get-tuple-element.858) | copy-start | bytes 12292
  96.6 171.1 %all-gather.15.cloned.1.call-start = ((), (), s32[]{:S(2)}) async-start(), calls=%async_computation.11 | async-start | bytes 1081344 | tf_op jit(solution)/shard_map/all_gather | solution.py:102
  97.3 194.4 %reduce-scatter.15.cloned.1.call-start = ((), (), s32[]{:S(2)}) async-start(), calls=%async_computation.10 | async-start | bytes 1966080 | tf_op jit(solution)/shard_map/reduce_scatter | solution.py:224
  266.0 107.0 %all-gather.17.cloned.1.call-start = ((), (), s32[]{:S(2)}) async-start(), calls=%async_computation.12 | async-start | bytes 8650752 | tf_op jit(solution)/shard_map/all_gather | solution.py:103
  266.8 186.0 %all-gather.19.cloned.1.call-start = ((), (), s32[]{:S(2)}) async-start(), calls=%async_computation.13 | async-start | bytes 8650752 | tf_op jit(solution)/shard_map/all_gather | solution.py:104
  267.6 243.4 %all-gather.21.cloned.1.call-start = ((), (), s32[]{:S(2)}) async-start(), calls=%async_computation.14 | async-start | bytes 3932160 | tf_op jit(solution)/shard_map/all_gather | solution.py:257
  293.7 184.2 %copy-start.7 = (f32[384,1024]{1,0:T(8,128)}, f32[384,1024]{1,0:T(8,128)S(1)}, u32[]{:S(2)}) copy-start(f32[384,1024]{1,0:T(8,128)S(1)} %get-tuple-element.866) | copy-start | bytes 4718596
  293.7 184.2 %copy-start.59 = (f32[384]{0:T(512)}, f32[384]{0:T(512)S(1)}, u32[]{:S(2)}) copy-start(f32[384]{0:T(512)S(1)} %broadcast_multiply_fusion.2) | copy-start | bytes 4612
  294.0 183.9 %copy-start.61 = (f32[384]{0:T(512)}, f32[384]{0:T(512)S(1)}, u32[]{:S(2)}) copy-start(f32[384]{0:T(512)S(1)} %fusion.103) | copy-start | bytes 4612
  483.0 196.4 %reduce-scatter.17.cloned.1.call-start = ((), (), s32[]{:S(2)}) async-start(), calls=%async_computation.15 | async-start | bytes 1966080 | tf_op jit(solution)/shard_map/reduce_scatter | solution.py:317
  619.0 167.0 %reduce-scatter.19.cloned.1.call-start = ((), (), s32[]{:S(2)}) async-start(), calls=%async_computation.16 | async-start | bytes 2162688 | tf_op jit(solution)/shard_map/reduce_scatter | solution.py:357
  622.4 296.2 %reduce-scatter.27.cloned.1.call-start = ((), (), s32[]{:S(2)}) async-start(), calls=%async_computation.20 | async-start | bytes 540672
  684.4 367.0 %reduce-scatter.29.cloned.1.call-start = ((), (), s32[]{:S(2)}) async-start(), calls=%async_computation.21 | async-start | bytes 540672
  686.2 482.1 %reduce-scatter.25.cloned.1.call-start = ((), (), s32[]{:S(2)}) async-start(), calls=%async_computation.19 | async-start | bytes 6488064 | tf_op jit(solution)/shard_map/reduce_scatter | solution.py:356
  700.6 652.3 %reduce-scatter.21.cloned.1.call-start = ((), (), s32[]{:S(2)}) async-start(), calls=%async_computation.17 | async-start | bytes 17301504 | tf_op jit(solution)/shard_map/reduce_scatter | solution.py:358
  712.2 827.5 %reduce-scatter.23.cloned.1.call-start = ((), (), s32[]{:S(2)}) async-start(), calls=%async_computation.18 | async-start | bytes 17301504 | tf_op jit(solution)/shard_map/reduce_scatter | solution.py:359
  787.5 755.9 %copy-start.15 = (f32[384,1024]{1,0:T(8,128)S(1)}, f32[384,1024]{1,0:T(8,128)}, u32[]{:S(2)}) copy-start(f32[384,1024]{1,0:T(8,128)} %copy-done.14) | copy-start | bytes 4718596
  787.5 755.9 %copy-start.75 = (f32[384]{0:T(512)S(1)}, f32[384]{0:T(512)}, u32[]{:S(2)}) copy-start(f32[384]{0:T(512)} %copy-done.74) | copy-start | bytes 4612
  790.8 752.6 %copy-start.18 = (bf16[24,16,1024]{2,1,0:T(8,128)(2,1)S(1)}, bf16[24,16,1024]{2,1,0:T(8,128)(2,1)}, u32[]{:S(2)}) copy-start(bf16[24,16,1024]{2,1,0:T(8,128)(2,1)} %param.33) | copy-start | bytes 2359300
  1354.7 235.6 %copy-start.37 = (f32[32,1536]{1,0:T(8,128)S(1)}, f32[32,1536]{1,0:T(8,128)}, u32[]{:S(2)}) copy-start(f32[32,1536]{1,0:T(8,128)} %param.34) | copy-start | bytes 589828
  1354.7 235.6 %copy-start.40 = (f32[32,1536]{1,0:T(8,128)S(1)}, f32[32,1536]{1,0:T(8,128)}, u32[]{:S(2)}) copy-start(f32[32,1536]{1,0:T(8,128)} %reduce-scatter.25.cloned.1.call-done) | copy-start | bytes 589828
  (78 other events, 1058.1 us)
Sparse Core Ops, SparseCore 0:
  11.5 61.7 all-gather.10
  96.7 17.0 all-gather.12
  117.3 53.6 all-gather.14
  266.1 25.5 reduce-scatter.14
  295.4 77.5 all-gather.16
  376.7 76.1 all-gather.18
  483.1 27.8 all-gather.20
  619.1 27.9 reduce-scatter.16
  649.3 136.6 reduce-scatter.18
  788.7 129.8 reduce-scatter.26
  921.5 129.9 reduce-scatter.28
  1057.9 110.4 reduce-scatter.24
  1170.7 182.1 reduce-scatter.20
  1355.1 184.5 reduce-scatter.22
where the time goes:
time: 1610 us
  waiting for transfers between devices  958 us (60%)
  matrix products  213 us (13%)
  local copies, waits for them, and re-layouts  142 us (9%)
  blocking collectives  141 us (9%)
  other arithmetic  117 us (7%)
  between operations  21.1 us (1%)
    unnamed x16, waiting for transfers between devices  260 us
    reduce_scatter x1, waiting for transfers between devices, shards(): lax.psum_scatter(grad_shrink, ('img', 'lat'), scatter_dimension=0, tiled=...  184 us
    reduce_scatter x1, waiting for transfers between devices, shards(): lax.psum_scatter(grad_expand, ('img', 'lat'), scatter_dimension=0, tiled=...  181 us
    reduce_scatter x1, waiting for transfers between devices, shards(): lax.psum_scatter(grad_attend, ('img', 'lat'), scatter_dimension=0, tiled=...  115 us
    all_gather x1, waiting for transfers between devices, shards(): lax.all_gather(to_half(expand_weight), ('img', 'lat'), axis=0, tiled=True)  78.9 us
    all_gather x1, waiting for transfers between devices, shards(): lax.all_gather(to_half(shrink_weight), ('img', 'lat'), axis=0, tiled=True)  70.6 us
    dot_general x5, matrix products, matmul_right_t(): lax.dot_general(first_op, second_op, (((1,), (1,)), ((), ())), preferred_...  54.9 us
    all_gather x1, blocking collectives, shards(): lax.all_gather(to_half(layer_biases), ('img', 'lat'), axis=0, tiled=True)  43.3 us
  transfers between devices with their start and end apart: 14, of which 10 were waited for; matrix products, arithmetic and copies ran while one was open for 20% of the time, Pallas kernels for 0%

commit v1 on v0

v1 whole, which is shorter than its diff:
```python
import functools
import math

import jax
import jax.numpy as jnp
from jax import lax
from jax.experimental import pallas as pl
from jax.experimental.pallas import tpu as pltpu
from jax.sharding import PartitionSpec as P

HEADS = 8
HDIM = 64
PATCH_IMG = 256
GROUP = 4
EPS = 1e-05
MOMENTUM = 0.9
DECAY = 0.0001
AVERAGING = 0.6
CLIP_NORM = 1.0
RATE_SCALES = (1.0, 100.0, 1.0, 1.0, 15.0, 1.0)
AXES = ("img", "lat")
LANES = 128
BLOCKS = 32
SCALE = HDIM ** (-0.5)
F32 = jnp.float32
BF16 = jnp.bfloat16
MESH = pl.DeviceIdType.MESH
VMEM_LIMIT = 60 * 1024 * 1024


def mm(a, b):
    return jnp.dot(a, b, preferred_element_type=F32)


def mm_tn(a, b):
    return lax.dot_general(a, b, (((0,), (0,)), ((), ())), preferred_element_type=F32)


def mm_nt(a, b):
    return lax.dot_general(a, b, (((1,), (1,)), ((), ())), preferred_element_type=F32)


def any_spec():
    return pl.BlockSpec(memory_space=pl.ANY)


def vmem_spec():
    return pl.BlockSpec(memory_space=pltpu.VMEM)


def params(**more):
    return pltpu.CompilerParams(vmem_limit_bytes=VMEM_LIMIT, **more)


def place():
    img = lax.axis_index("img")
    lat = lax.axis_index("lat")
    return img // 2, img % 2, lat // 2, lat % 2


def flat(a, b, e, c):
    return ((a * 2 + b) * 2 + e) * 2 + c


def device(a, b, e, c):
    return (a * 2 + b, e * 2 + c)


def first_partner(a, b, e, c):
    return a, (b + 1 - c) % 2, (e + c) % 2, c


def second_partner(a, b, e, c):
    return a, (b + c) % 2, (e + 1 - c) % 2, c


def z_order(depth):
    order = [0]
    for k in range(1, depth // 2 + 1):
        order.append(k)
        if depth - k != k:
            order.append(depth - k)
    return order


def greet(depth, a, b, e, c):
    barrier = pltpu.get_barrier_semaphore()
    friends = [device((a + k) % depth, b, e, c) for k in range(1, depth)]
    friends += [
        device(*first_partner(a, b, e, c)),
        device(*second_partner(a, b, e, c)),
        device(a, b, e, 1 - c),
    ]
    for friend in friends:
        pl.semaphore_signal(barrier, inc=1, device_id=friend, device_id_type=MESH)
    pl.semaphore_wait(barrier, len(friends))


def gather_kernel(depth, x_ref, o_ref, local_sem, send_sem, recv_sem):
    a, b, e, c = place()
    me = flat(a, b, e, c)
    greet(depth, a, b, e, c)
    own = pltpu.make_async_copy(x_ref, o_ref.at[me], local_sem)
    own.start()
    one = first_partner(a, b, e, c)
    two = second_partner(a, b, e, c)
    both = second_partner(*one)
    homes = [(a, b, e, c), one, two, both]
    twin = device(a, b, e, 1 - c)
    sends = []

    def source(k, j):
        _, hb, he, hc = homes[j % 4]
        return flat((a - k) % depth, hb, he, hc if j < 4 else 1 - c)

    def send(k, j, src, row, target):
        slot = k * 8 + j
        copy = pltpu.make_async_remote_copy(
            src_ref=src,
            dst_ref=o_ref.at[row],
            send_sem=send_sem.at[slot],
            recv_sem=recv_sem.at[slot],
            device_id=target,
            device_id_type=MESH,
        )
        copy.start()
        sends.append(copy)

    def arrive(k, j):
        slot = k * 8 + j
        pltpu.make_async_remote_copy(
            src_ref=x_ref,
            dst_ref=o_ref.at[source(k, j)],
            send_sem=send_sem.at[slot],
            recv_sem=recv_sem.at[slot],
            device_id=twin,
            device_id_type=MESH,
        ).wait_recv()

    def block(k, j):
        return x_ref if (k, j) == (0, 0) else o_ref.at[source(k, j)]

    def stage_one(k):
        if k:
            arrive(k, 0)
        row = source(k, 0)
        send(k, 1, block(k, 0), row, device(*one))
        send(k, 2, block(k, 0), row, device(*two))
        send(k, 4, block(k, 0), row, twin)

    def stage_two(k):
        arrive(k, 1)
        send(k, 3, block(k, 1), source(k, 1), device(*two))
        send(k, 5, block(k, 1), source(k, 1), twin)
        arrive(k, 2)
        send(k, 6, block(k, 2), source(k, 2), twin)

    def stage_three(k):
        arrive(k, 3)
        send(k, 7, block(k, 3), source(k, 3), twin)

    order = z_order(depth)
    for k in order[1:]:
        send(k, 0, x_ref, me, device((a + k) % depth, b, e, c))
    for n in range(depth + 2):
        if n < depth:
            stage_one(order[n])
        if 1 <= n < depth + 1:
            stage_two(order[n - 1])
        if n >= 2:
            stage_three(order[n - 2])
    for k in range(depth):
        for j in range(4, 8):
            arrive(k, j)
    for copy in sends:
        copy.wait_send()
    own.wait()


def gather_fast(shard, depth, collective_id):
    count = depth * 8
    return pl.pallas_call(
        functools.partial(gather_kernel, depth),
        out_shape=jax.ShapeDtypeStruct((count,) + shard.shape, shard.dtype),
        in_specs=[any_spec()],
        out_specs=any_spec(),
        scratch_shapes=[
            pltpu.SemaphoreType.DMA,
            pltpu.SemaphoreType.DMA((count,)),
            pltpu.SemaphoreType.DMA((count,)),
        ],
        compiler_params=pltpu.CompilerParams(collective_id=collective_id, has_side_effects=True),
        name=f"gather{collective_id}",
    )(shard)


def add_into(target, first, second, rows, chunk):
    @pl.loop(0, rows // chunk)
    def _(step):
        part = pl.ds(step * chunk, chunk)
        total = first[part, :].astype(F32) + second[part, :].astype(F32)
        target[part, :] = total.astype(target.dtype)


def scatter_kernel(
    depth, chunk, g_ref, o_ref, own, from_c, from_two, from_one, from_z, load_sem, send_sem, recv_sem
):
    a, b, e, c = place()
    rows = o_ref.shape[0]
    one = first_partner(a, b, e, c)
    two = second_partner(a, b, e, c)
    both = second_partner(*one)
    homes = [(a, b, e, c), one, two, both]
    twin = device(a, b, e, 1 - c)
    order = z_order(depth)
    order = order[1:] + order[:1]
    sends = []

    def target_row(k, j, core):
        _, hb, he, _ = homes[j]
        return flat((a + k) % depth, hb, he, core)

    def remote(slot, src, dst, target):
        return pltpu.make_async_remote_copy(
            src_ref=src,
            dst_ref=dst,
            send_sem=send_sem.at[slot],
            recv_sem=recv_sem.at[slot],
            device_id=target,
            device_id_type=MESH,
        )

    def send(slot, src, dst, target):
        copy = remote(slot, src, dst, target)
        copy.start()
        sends.append(copy)

    loads = {}
    for k in order:
        for j in (3, 2, 1, 0):
            copy = pltpu.make_async_copy(
                g_ref.at[target_row(k, j, c)], own.at[k * 4 + j], load_sem.at[k * 4 + j]
            )
            copy.start()
            loads[k, j] = copy
    greet(depth, a, b, e, c)
    for k in order:
        for j in (3, 2, 1, 0):
            there = (0, 2, 1, 3)[j]
            send(k * 8 + j, g_ref.at[target_row(k, there, 1 - c)], from_c.at[k * 4 + j], twin)

    def stage_c(k):
        for j in (3, 2, 1, 0):
            loads[k, j].wait()
            remote(k * 8 + j, own.at[k * 4 + j], from_c.at[k * 4 + j], twin).wait_recv()
            add_into(own.at[k * 4 + j], own.at[k * 4 + j], from_c.at[k * 4 + j], rows, chunk)
            if j >= 2:
                send(k * 8 + 2 + j, own.at[k * 4 + j], from_two.at[k * 2 + j - 2], device(*two))

    def stage_two(k):
        for j in (3, 2):
            spot = from_two.at[k * 2 + j - 2]
            remote(k * 8 + 2 + j, own.at[k * 4 + j], spot, device(*two)).wait_recv()
            add_into(own.at[k * 4 + j - 2], own.at[k * 4 + j - 2], spot, rows, chunk)
            if j == 3:
                send(k * 8 + 6, own.at[k * 4 + 1], from_one.at[k], device(*one))

    def stage_one(k):
        spot = from_one.at[k]
        remote(k * 8 + 6, own.at[k * 4 + 1], spot, device(*one)).wait_recv()
        if k:
            add_into(own.at[k * 4], own.at[k * 4], spot, rows, chunk)
            send(k * 8 + 7, own.at[k * 4], from_z.at[k - 1], device((a + k) % depth, b, e, c))

    for n in range(depth + 2):
        if n < depth:
            stage_c(order[n])
        if 1 <= n < depth + 1:
            stage_two(order[n - 1])
        if n >= 2:
            stage_one(order[n - 2])
    for k in range(1, depth):
        remote(k * 8 + 7, own.at[k * 4], from_z.at[k - 1], twin).wait_recv()

    @pl.loop(0, rows // chunk)
    def _(step):
        part = pl.ds(step * chunk, chunk)
        total = own[0, part, :].astype(F32) + from_one[0, part, :].astype(F32)
        for k in range(1, depth):
            total = total + from_z[k - 1, part, :].astype(F32)
        o_ref[part, :] = total

    for copy in sends:
        copy.wait_send()


def scatter_fast(parts, depth, collective_id, chunk):
    _, rows, cols = parts.shape
    count = depth * 8

    def slots(n):
        return pltpu.VMEM((n, rows, cols), parts.dtype)

    return pl.pallas_call(
        functools.partial(scatter_kernel, depth, chunk),
        out_shape=jax.ShapeDtypeStruct((rows, cols), F32),
        in_specs=[any_spec()],
        out_specs=vmem_spec(),
        scratch_shapes=[
            slots(depth * 4),
            slots(depth * 4),
            slots(depth * 2),
            slots(depth),
            slots(depth - 1),
            pltpu.SemaphoreType.DMA((depth * 4,)),
            pltpu.SemaphoreType.DMA((count,)),
            pltpu.SemaphoreType.DMA((count,)),
        ],
        compiler_params=params(collective_id=collective_id, has_side_effects=True),
        name=f"scatter{collective_id}",
    )(parts)


def total_kernel(images, lats, x_ref, o_ref, slots, send_sem, recv_sem):
    img = lax.axis_index("img")
    lat = lax.axis_index("lat")
    count = images * lats
    me = img * lats + lat
    barrier = pltpu.get_barrier_semaphore()
    for k in range(1, count):
        there = (me + k) % count
        pl.semaphore_signal(
            barrier, inc=1, device_id=(there // lats, there % lats), device_id_type=MESH
        )
    pl.semaphore_wait(barrier, count - 1)
    slots[me] = x_ref[...]
    copies = []
    for k in range(1, count):
        there = (me + k) % count
        copy = pltpu.make_async_remote_copy(
            src_ref=x_ref,
            dst_ref=slots.at[me],
            send_sem=send_sem.at[k],
            recv_sem=recv_sem.at[k],
            device_id=(there // lats, there % lats),
            device_id_type=MESH,
        )
        copy.start()
        copies.append(copy)
    for k in range(1, count):
        pltpu.make_async_remote_copy(
            src_ref=x_ref,
            dst_ref=slots.at[(me - k) % count],
            send_sem=send_sem.at[k],
            recv_sem=recv_sem.at[k],
            device_id=(img, lat),
            device_id_type=MESH,
        ).wait_recv()
    o_ref[...] = jnp.sum(slots[...], axis=0)
    for copy in copies:
        copy.wait_send()


def total_fast(tile, images, lats, collective_id):
    count = images * lats
    return pl.pallas_call(
        functools.partial(total_kernel, images, lats),
        out_shape=jax.ShapeDtypeStruct(tile.shape, tile.dtype),
        in_specs=[vmem_spec()],
        out_specs=vmem_spec(),
        scratch_shapes=[
            pltpu.VMEM((count,) + tile.shape, tile.dtype),
            pltpu.SemaphoreType.DMA((count,)),
            pltpu.SemaphoreType.DMA((count,)),
        ],
        compiler_params=pltpu.CompilerParams(collective_id=collective_id, has_side_effects=True),
        name=f"total{collective_id}",
    )(tile)


def normalise(values):
    center = values - jnp.mean(values, axis=-1, keepdims=True)
    spread = jnp.mean(center * center, axis=-1, keepdims=True)
    scale = lax.rsqrt(spread + EPS)
    return center * scale, scale


def norm_back(grad, hat, scale, gain):
    inner = grad * gain
    first = jnp.mean(inner, axis=-1, keepdims=True)
    second = jnp.mean(inner * hat, axis=-1, keepdims=True)
    return scale * (inner - first - hat * second)


def media_kernel(m_ref, gb_ref, wk_ref, wv_ref, k_ref, v_ref):
    hat, _ = normalise(m_ref[...].astype(F32))
    normed = (hat * gb_ref[0:1, :] + gb_ref[3:4, :]).astype(BF16)
    k_ref[...] = mm(normed, wk_ref[...]).astype(BF16)
    v_ref[...] = mm(normed, wv_ref[...]).astype(BF16)


def media_project(media, gains, attend, inner):
    rows, width = media.shape
    out = jax.ShapeDtypeStruct((rows, inner), BF16)
    block = pl.BlockSpec((PATCH_IMG, inner), lambda i: (i, 0))
    return pl.pallas_call(
        media_kernel,
        grid=(rows // PATCH_IMG,),
        out_shape=(out, out),
        in_specs=[
            pl.BlockSpec((PATCH_IMG, width), lambda i: (i, 0)),
            pl.BlockSpec(gains.shape, lambda i: (0, 0)),
            pl.BlockSpec((width, inner), lambda i: (0, 1)),
            pl.BlockSpec((width, inner), lambda i: (0, 2)),
        ],
        out_specs=(block, block),
        compiler_params=params(),
        cost_estimate=pl.CostEstimate(
            flops=4 * rows * width * inner, bytes_accessed=4 * rows * width, transcendentals=0
        ),
        name="media_project",
    )(media, gains, attend, attend)


def latent_kernel(l_ref, gb_ref, w_ref, q_ref, k_ref, v_ref):
    inner = q_ref.shape[1]
    hat, _ = normalise(l_ref[...])
    normed = (hat * gb_ref[1:2, :] + gb_ref[4:5, :]).astype(BF16)
    q_ref[...] = mm(normed, w_ref[:, :inner]).astype(BF16)
    k_ref[...] = mm(normed, w_ref[:, inner : 2 * inner]).astype(BF16)
    v_ref[...] = mm(normed, w_ref[:, 2 * inner : 3 * inner]).astype(BF16)


def latent_project(latents, gains, attend, inner):
    out = jax.ShapeDtypeStruct((latents.shape[0], inner), BF16)
    return pl.pallas_call(
        latent_kernel,
        out_shape=(out, out, out),
        in_specs=[vmem_spec()] * 3,
        out_specs=(vmem_spec(),) * 3,
        compiler_params=params(),
        name="latent_project",
    )(latents, gains, attend)


def head_mask(kind):
    rows = lax.broadcasted_iota(jnp.int32, (GROUP * HDIM, GROUP * HDIM), 0) // HDIM
    cols = lax.broadcasted_iota(jnp.int32, (GROUP * HDIM, GROUP * HDIM), 1) // HDIM
    return (rows == cols).astype(F32).astype(kind)


def spread_heads(queries, group, mask):
    width = GROUP * HDIM
    part = queries[:, group * width : (group + 1) * width]
    return jnp.concatenate([part] * GROUP, axis=0) * mask


def take_heads(full, mask):
    total = None
    for h in range(GROUP):
        part = slice(h * HDIM, (h + 1) * HDIM)
        term = full[part, :] * mask[part, :]
        total = term if total is None else total + term
    return total


def pack_columns(columns, first=0):
    rows = columns[0].shape[0]
    lane = lax.broadcasted_iota(jnp.int32, (rows, LANES), 1)
    tile = jnp.zeros((rows, LANES), F32)
    for h, column in enumerate(columns):
        tile = jnp.where(lane == first + h, column, tile)
    return tile


def expand_columns(tile, width):
    rows = tile.shape[0]
    head = lax.broadcasted_iota(jnp.int32, (rows, width), 1) // HDIM
    out = jnp.zeros((rows, width), F32)
    for h in range(width // HDIM):
        out = jnp.where(head == h, tile[:, h : h + 1], out)
    return out


def forward_kernel(
    ids, q0, q1, q2, q3, k_ref, v_ref, kl_ref, vl_ref, keep, send, keep_st, send_st, acc, tops, sums
):
    step = pl.program_id(0)
    clips = acc.shape[0]
    inner = acc.shape[2]
    groups = inner // (GROUP * HDIM)
    width = GROUP * HDIM
    mask = head_mask(F32)
    mask_half = mask.astype(BF16)

    def clip_queries(clip):
        parts = [q[clip] for q in (q0, q1, q2, q3)]
        return jnp.concatenate(parts, axis=0) * BF16(SCALE)

    def attend(clip, keys, values, fresh):
        queries = clip_queries(clip)
        new_tops, new_sums = [], []
        for g in range(groups):
            cols = slice(g * width, (g + 1) * width)
            scores = mm_nt(spread_heads(queries, g, mask_half), keys[:, cols])
            top = jnp.max(scores, axis=-1, keepdims=True)
            if not fresh:
                old_tile = tops[clip]
                old_top = jnp.concatenate(
                    [old_tile[:, g * GROUP + h : g * GROUP + h + 1] for h in range(GROUP)], axis=0
                )
                top = jnp.maximum(top, old_top)
            probs = jnp.exp(scores - top)
            total = jnp.sum(probs, axis=-1, keepdims=True)
            part = take_heads(mm(probs.astype(BF16), values[:, cols]), mask)
            if not fresh:
                old_tile = sums[clip]
                old_sum = jnp.concatenate(
                    [old_tile[:, g * GROUP + h : g * GROUP + h + 1] for h in range(GROUP)], axis=0
                )
                shrink = jnp.exp(old_top - top)
                total = total + old_sum * shrink
                part = part + acc[clip, :, cols] * take_heads(shrink, mask)
            acc[clip, :, cols] = part
            for h in range(GROUP):
                new_tops.append(top[h * HDIM : (h + 1) * HDIM])
                new_sums.append(total[h * HDIM : (h + 1) * HDIM])
        tops[clip] = pack_columns(new_tops)
        sums[clip] = pack_columns(new_sums)

    @pl.when(step == 0)
    def _():
        @pl.loop(0, clips)
        def _(clip):
            attend(clip, kl_ref[clip], vl_ref[clip], True)

    attend(ids[step], k_ref[...], v_ref[...], False)

    @pl.when(step == pl.num_programs(0) - 1)
    def _():
        rows = keep.shape[2]
        lane = lax.broadcasted_iota(jnp.int32, (HDIM, LANES), 1)

        @pl.loop(0, clips)
        def _(clip):
            total = jnp.where(lane < HEADS, sums[clip], 1.0)
            stat = tops[clip] + jnp.log(total)
            out = (acc[clip] / expand_columns(total, inner)).astype(BF16)
            for r in range(4):
                part = slice(r * rows, (r + 1) * rows)
                where_o, where_s = (send, send_st) if r % 2 else (keep, keep_st)
                where_o[r // 2, clip] = out[part]
                where_s[r // 2, clip] = stat[part]


def attention_forward(ids, queries, keys, values, latent_keys, latent_values):
    clips, rows, inner = queries[0].shape
    frames = keys.shape[0] // PATCH_IMG
    out = jax.ShapeDtypeStruct((2, clips, rows, inner), BF16)
    stat = jax.ShapeDtypeStruct((2, clips, rows, LANES), F32)
    block = pl.BlockSpec((PATCH_IMG, inner), lambda i, ids: (i, 0))

    def whole(shape):
        return pl.BlockSpec(shape, lambda i, ids: (0,) * len(shape))

    return pl.pallas_call(
        forward_kernel,
        grid_spec=pltpu.PrefetchScalarGridSpec(
            num_scalar_prefetch=1,
            grid=(frames,),
            in_specs=[whole((clips, rows, inner))] * 4
            + [block, block]
            + [whole((clips, rows, inner))] * 2,
            out_specs=(whole(out.shape), whole(out.shape), whole(stat.shape), whole(stat.shape)),
            scratch_shapes=[
                pltpu.VMEM((clips, 4 * rows, inner), F32),
                pltpu.VMEM((clips, 4 * rows, LANES), F32),
                pltpu.VMEM((clips, 4 * rows, LANES), F32),
            ],
        ),
        out_shape=(out, out, stat, stat),
        compiler_params=params(),
        name="attention_forward",
    )(ids, *queries, keys, values, latent_keys, latent_values)


def join_partials(first, first_stat, second, second_stat):
    width = first.shape[-1]
    top = jnp.maximum(first_stat, second_stat)
    total = jnp.exp(first_stat - top) + jnp.exp(second_stat - top)
    stat = top + jnp.log(total)
    out = first.astype(F32) * expand_columns(jnp.exp(first_stat - stat), width)
    out = out + second.astype(F32) * expand_columns(jnp.exp(second_stat - stat), width)
    return out, stat


def join_kernel(keep, keep_st, got, got_st, own, own_st, away, away_st):
    out, stat = join_partials(keep[0], keep_st[0], got[0], got_st[0])
    own[...] = out
    own_st[...] = stat
    out, stat = join_partials(keep[1], keep_st[1], got[1], got_st[1])
    away[...] = out.astype(BF16)
    away_st[...] = stat


def join_cores(keep, keep_st, got, got_st):
    _, rows, inner = keep.shape
    stat = jax.ShapeDtypeStruct((rows, LANES), F32)
    return pl.pallas_call(
        join_kernel,
        out_shape=(
            jax.ShapeDtypeStruct((rows, inner), F32),
            stat,
            jax.ShapeDtypeStruct((rows, inner), BF16),
            stat,
        ),
        in_specs=[vmem_spec()] * 4,
        out_specs=(vmem_spec(),) * 4,
        compiler_params=params(),
        name="join_cores",
    )(keep, keep_st, got, got_st)


def feed_kernel(
    own,
    own_st,
    got,
    got_st,
    lat_ref,
    cot_ref,
    gb_ref,
    w_ref,
    out_ref,
    mixed_grad,
    context_grad,
    tile_ref,
    gain_ref,
    gw_ref,
    expand_v,
    shrink_v,
    output_v,
    grad_e,
    grad_s,
    grad_o,
    normed_v,
    normed_t,
    hat_v,
    acc_g,
    load_sem,
    store_sem,
):
    groups = expand_v.shape[0]
    width = expand_v.shape[3]
    blocks = expand_v.shape[1]
    shrink_rows = shrink_v.shape[1]
    per_group = blocks // groups
    expand_rows = expand_v.shape[2]
    shrink_at = groups * expand_rows
    output_at = shrink_at + shrink_rows
    output_rows = output_v.shape[1]
    half = width // 2
    inner = own.shape[1]

    def load_expand(g):
        return pltpu.make_async_copy(
            w_ref.at[:, pl.ds(g * expand_rows, expand_rows), :], expand_v.at[g], load_sem.at[g]
        )

    def load_shrink(g):
        part = pl.ds(g * per_group, per_group)
        return pltpu.make_async_copy(
            w_ref.at[part, pl.ds(shrink_at, shrink_rows), :],
            shrink_v.at[part],
            load_sem.at[groups + g],
        )

    load_output = pltpu.make_async_copy(
        w_ref.at[:, pl.ds(output_at, output_rows), :], output_v, load_sem.at[2 * groups]
    )
    load_output.start()
    for g in range(groups):
        load_expand(g).start()
        load_shrink(g).start()

    context, stat = join_partials(own[...], own_st[...], got[...], got_st[...])
    context_half = context.astype(BF16)
    load_output.wait()
    weight_o = output_v[...].reshape(inner, width)
    mixed = lat_ref[...] + mm(context_half, weight_o)
    hat, scale = normalise(mixed)
    hat_v[...] = hat
    normed = (hat * gb_ref[2:3, :] + gb_ref[5:6, :]).astype(BF16)
    normed_v[...] = normed
    normed_t[...] = normed.astype(F32).T.astype(BF16)
    out_ref[...] = mixed
    acc_g[...] = jnp.zeros_like(acc_g)

    def store_e(s, slot):
        return pltpu.make_async_copy(
            grad_e.at[slot],
            gw_ref.at[:, pl.ds((s // 2) * expand_rows, expand_rows), pl.ds((s % 2) * half, half)],
            store_sem.at[slot],
        )

    def store_s(s, slot):
        rows = half // shrink_rows
        return pltpu.make_async_copy(
            grad_s.at[slot],
            gw_ref.at[pl.ds(s * rows, rows), pl.ds(shrink_at, shrink_rows), :],
            store_sem.at[2 + slot],
        )

    cot = cot_ref[...]
    steps = 2 * groups
    for s in range(steps):
        g, slot = s // 2, s % 2
        if slot == 0:
            load_expand(g).wait()
            load_shrink(g).wait()
        cols = slice(slot * half, (slot + 1) * half)
        w_e = expand_v[g, :, :, cols].reshape(blocks * expand_rows, half)
        first = s * half // shrink_rows
        w_s = shrink_v[first : first + half // shrink_rows].reshape(half, width)
        pre = mm(normed_v[...], w_e)
        cdf = 0.5 * (1.0 + lax.erf(pre * (0.5**0.5)))
        hidden = (pre * cdf).astype(BF16)
        out_ref[...] += mm(hidden, w_s)
        grad_hidden = mm_nt(cot, w_s)
        pdf = jnp.exp(-0.5 * pre * pre) * (1.0 / math.sqrt(2.0 * math.pi))
        grad_pre = (grad_hidden * (cdf + pre * pdf)).astype(BF16)
        if s >= 2:
            store_e(s - 2, slot).wait()
            store_s(s - 2, slot).wait()
        grad_s[slot] = mm_tn(hidden, cot).astype(BF16).reshape(half // shrink_rows, shrink_rows, width)
        grad_e[slot] = (
            mm(normed_t[...], grad_pre).astype(BF16).reshape(blocks, expand_rows, half)
        )
        store_e(s, slot).start()
        store_s(s, slot).start()
        acc_g[...] += mm_nt(grad_pre, w_e)

    grad_normed = acc_g[...]
    hat = hat_v[...]
    rows = gain_ref.shape[0]
    gain_ref[...] = jnp.concatenate(
        [
            jnp.sum(grad_normed * hat, axis=0, keepdims=True),
            jnp.sum(grad_normed, axis=0, keepdims=True),
            jnp.zeros((rows - 2, width), F32),
        ],
        axis=0,
    )
    total = cot.astype(F32) + norm_back(grad_normed, hat, scale, gb_ref[2:3, :])
    mixed_grad[...] = total
    attended = total.astype(BF16)
    grad_o[...] = mm_tn(context_half, attended).astype(BF16).reshape(grad_o.shape)
    store_o = pltpu.make_async_copy(
        grad_o, gw_ref.at[:, pl.ds(output_at, output_rows), :], store_sem.at[4]
    )
    store_o.start()
    grad_c = mm_nt(attended, weight_o).astype(BF16)
    context_grad[...] = grad_c
    product = grad_c.astype(F32) * context
    head = lax.broadcasted_iota(jnp.int32, product.shape, 1) // HDIM
    deltas = [
        jnp.sum(jnp.where(head == h, product, 0.0), axis=-1, keepdims=True) for h in range(HEADS)
    ]
    lane = lax.broadcasted_iota(jnp.int32, stat.shape, 1)
    tile_ref[...] = jnp.where(lane < HEADS, stat, pack_columns(deltas, HEADS))
    for s in range(steps - 2, steps):
        store_e(s, s % 2).wait()
        store_s(s, s % 2).wait()
    store_o.wait()


def feed_forward(own, own_st, got, got_st, latents, cotangent, gains, weights):
    rows, width = latents.shape
    inner = own.shape[1]
    blocks = weights.shape[0]
    ff = 4 * width
    groups = ff // width
    expand_rows = width // blocks
    shrink_rows = ff // blocks
    output_rows = inner // blocks
    half = width // 2
    flops = 2 * rows * (6 * width * ff + 3 * width * inner)
    return pl.pallas_call(
        feed_kernel,
        out_shape=(
            jax.ShapeDtypeStruct((rows, width), F32),
            jax.ShapeDtypeStruct((rows, width), F32),
            jax.ShapeDtypeStruct((rows, inner), BF16),
            jax.ShapeDtypeStruct((rows, LANES), F32),
            jax.ShapeDtypeStruct((8, width), F32),
            jax.ShapeDtypeStruct(weights.shape, BF16),
        ),
        in_specs=[vmem_spec()] * 7 + [any_spec()],
        out_specs=(vmem_spec(),) * 5 + (any_spec(),),
        scratch_shapes=[
            pltpu.VMEM((groups, blocks, expand_rows, width), BF16),
            pltpu.VMEM((blocks, shrink_rows, width), BF16),
            pltpu.VMEM((blocks, output_rows, width), BF16),
            pltpu.VMEM((2, blocks, expand_rows, half), BF16),
            pltpu.VMEM((2, half // shrink_rows, shrink_rows, width), BF16),
            pltpu.VMEM((blocks, output_rows, width), BF16),
            pltpu.VMEM((rows, width), BF16),
            pltpu.VMEM((width, rows), BF16),
            pltpu.VMEM((rows, width), F32),
            pltpu.VMEM((rows, width), F32),
            pltpu.SemaphoreType.DMA((2 * groups + 1,)),
            pltpu.SemaphoreType.DMA((5,)),
        ],
        compiler_params=params(),
        cost_estimate=pl.CostEstimate(
            flops=flops, bytes_accessed=4 * weights.size, transcendentals=2 * rows * ff
        ),
        name="feed_forward",
    )(own, own_st, got, got_st, latents, cotangent, gains, weights)


def backward_kernel(
    ids,
    q0,
    q1,
    q2,
    q3,
    g0,
    g1,
    g2,
    g3,
    t0,
    t1,
    t2,
    t3,
    k_ref,
    v_ref,
    kl_ref,
    vl_ref,
    m_ref,
    gb_ref,
    wk_ref,
    wv_ref,
    media_grad,
    latent_kv,
    keep,
    send,
    weight_grad,
    gain_ref,
    acc,
):
    step = pl.program_id(0)
    clips = acc.shape[0]
    inner = acc.shape[2]
    groups = inner // (GROUP * HDIM)
    width = GROUP * HDIM
    mask = head_mask(F32)
    mask_half = mask.astype(BF16)

    def attend(clip, keys, values, fresh):
        queries = jnp.concatenate([q[clip] for q in (q0, q1, q2, q3)], axis=0) * BF16(SCALE)
        grads = jnp.concatenate([g[clip] for g in (g0, g1, g2, g3)], axis=0)
        stats = jnp.concatenate([t[clip] for t in (t0, t1, t2, t3)], axis=0).T
        key_parts, value_parts = [], []
        for g in range(groups):
            cols = slice(g * width, (g + 1) * width)

            def line(first):
                at = first + g * GROUP
                return jnp.concatenate([stats[at + h : at + h + 1, :] for h in range(GROUP)], axis=1)

            wide_q = spread_heads(queries, g, mask_half)
            wide_g = spread_heads(grads, g, mask_half)
            probs = jnp.exp(mm_nt(keys[:, cols], wide_q) - line(0))
            grad_probs = mm_nt(values[:, cols], wide_g)
            grad_scores = (probs * (grad_probs - line(HEADS))).astype(BF16)
            key_parts.append(mm(grad_scores, wide_q))
            value_parts.append(mm(probs.astype(BF16), wide_g))
            part = take_heads(mm_tn(grad_scores, keys[:, cols]), mask)
            if fresh:
                acc[clip, :, cols] = part
            else:
                acc[clip, :, cols] += part
        return jnp.concatenate(key_parts + value_parts, axis=1).astype(BF16)

    @pl.when(step == 0)
    def _():
        gain_ref[...] = jnp.zeros_like(gain_ref)
        weight_grad[...] = jnp.zeros_like(weight_grad)

        @pl.loop(0, clips)
        def _(clip):
            latent_kv[clip] = attend(clip, kl_ref[clip], vl_ref[clip], True)

    grad_kv = attend(ids[step], k_ref[...], v_ref[...], False)
    hat, scale = normalise(m_ref[...].astype(F32))
    gain = gb_ref[0:1, :]
    normed = (hat * gain + gb_ref[3:4, :]).astype(BF16)
    weight_grad[...] += mm_tn(normed, grad_kv)
    grad = mm_nt(grad_kv[:, :inner], wk_ref[...]) + mm_nt(grad_kv[:, inner:], wv_ref[...])
    gain_ref[0:1, :] += jnp.sum(grad * hat, axis=0, keepdims=True)
    gain_ref[1:2, :] += jnp.sum(grad, axis=0, keepdims=True)
    media_grad[...] = norm_back(grad, hat, scale, gain).astype(BF16)

    @pl.when(step == pl.num_programs(0) - 1)
    def _():
        rows = keep.shape[2]

        @pl.loop(0, clips)
        def _(clip):
            out = (acc[clip] * SCALE).astype(BF16)
            for r in range(4):
                part = slice(r * rows, (r + 1) * rows)
                where_o = send if r % 2 else keep
                where_o[r // 2, clip] = out[part]


def attention_backward(
    ids, queries, grads, tiles, keys, values, latent_keys, latent_values, media, gains, attend
):
    clips, rows, inner = queries[0].shape
    width = media.shape[1]
    frames = keys.shape[0] // PATCH_IMG
    block = pl.BlockSpec((PATCH_IMG, inner), lambda i, ids: (i, 0))
    wide = pl.BlockSpec((PATCH_IMG, width), lambda i, ids: (i, 0))

    def whole(shape):
        return pl.BlockSpec(shape, lambda i, ids: (0,) * len(shape))

    def column(n):
        return pl.BlockSpec((width, inner), lambda i, ids: (0, n))

    query = whole((clips, rows, inner))
    pair = (2, clips, rows, inner)
    return pl.pallas_call(
        backward_kernel,
        grid_spec=pltpu.PrefetchScalarGridSpec(
            num_scalar_prefetch=1,
            grid=(frames,),
            in_specs=[query] * 8
            + [whole((clips, rows, LANES))] * 4
            + [block, block, query, query, wide, whole(gains.shape), column(1), column(2)],
            out_specs=(
                wide,
                whole((clips, rows, 2 * inner)),
                whole(pair),
                whole(pair),
                whole((width, 2 * inner)),
                whole((8, width)),
            ),
            scratch_shapes=[pltpu.VMEM((clips, 4 * rows, inner), F32)],
        ),
        out_shape=(
            jax.ShapeDtypeStruct(media.shape, BF16),
            jax.ShapeDtypeStruct((clips, rows, 2 * inner), BF16),
            jax.ShapeDtypeStruct(pair, BF16),
            jax.ShapeDtypeStruct(pair, BF16),
            jax.ShapeDtypeStruct((width, 2 * inner), F32),
            jax.ShapeDtypeStruct((8, width), F32),
        ),
        compiler_params=params(),
        name="attention_backward",
    )(
        ids,
        *queries,
        *grads,
        *tiles,
        keys,
        values,
        latent_keys,
        latent_values,
        media,
        gains,
        attend,
        attend,
    )


def last_kernel(
    lat_ref, mixed_grad, first, second, kv_ref, gb_ref, w_ref, gw_ref, gm_ref, gf_ref, out_ref, pack_ref
):
    inner = first.shape[1]
    width = lat_ref.shape[1]
    hat, scale = normalise(lat_ref[...])
    gain = gb_ref[1:2, :]
    normed = (hat * gain + gb_ref[4:5, :]).astype(BF16)
    grad_q = (first[...].astype(F32) + second[...].astype(F32)).astype(BF16)
    grad_kv = kv_ref[...]
    grad = mm_nt(grad_q, w_ref[:, :inner]) + mm_nt(grad_kv, w_ref[:, inner : 3 * inner])
    pack_ref[:, :inner] = mm_tn(normed, grad_q).astype(BF16)
    pack_ref[:, inner : 3 * inner] = (gw_ref[...] + mm_tn(normed, grad_kv)).astype(BF16)
    lines = jnp.concatenate(
        [
            gm_ref[0:1, :],
            jnp.sum(grad * hat, axis=0, keepdims=True),
            gf_ref[0:1, :],
            gm_ref[1:2, :],
            jnp.sum(grad, axis=0, keepdims=True),
            gf_ref[1:2, :],
            jnp.zeros((LANES - 6, width), F32),
        ],
        axis=0,
    )
    pack_ref[:, 3 * inner :] = lines.T.astype(BF16)
    out_ref[...] = mixed_grad[...] + norm_back(grad, hat, scale, gain)


def latent_backward(latents, mixed_grad, first, second, grad_kv, gains, attend, grad_w, gain_m, gain_f):
    return pl.pallas_call(
        last_kernel,
        out_shape=(
            jax.ShapeDtypeStruct(latents.shape, F32),
            jax.ShapeDtypeStruct(attend.shape, BF16),
        ),
        in_specs=[vmem_spec()] * 10,
        out_specs=(vmem_spec(), vmem_spec()),
        compiler_params=params(),
        name="latent_backward",
    )(latents, mixed_grad, first, second, grad_kv, gains, attend, grad_w, gain_m, gain_f)


def pack_feed(expand, shrink, output):
    width = shrink.shape[-1]
    groups = expand.shape[-1] // width
    lead = expand.shape[:-2]
    rows = expand.shape[-2]
    cut = expand.reshape(lead + (rows, groups, width))
    cut = jnp.moveaxis(cut, -2, -3).reshape(lead + (groups * rows, width))
    return jnp.concatenate([cut, shrink, output], axis=-2)


def unpack_feed(packed, rows, shrink_rows):
    width = packed.shape[-1]
    lead = packed.shape[:-2]
    groups = (packed.shape[-2] - shrink_rows) // rows
    split = groups * rows
    cut = packed[..., :split, :].reshape(lead + (groups, rows, width))
    expand = jnp.moveaxis(cut, -3, -2).reshape(lead + (rows, groups * width))
    return (
        expand,
        packed[..., split : split + shrink_rows, :],
        packed[..., split + shrink_rows :, :],
    )


def step_size(width, inner, ff):
    return 0.37 * math.sqrt((4 * width * inner + 2 * width * ff) / width)


def lat_pairs(count, along_core):
    pairs = []
    for lat in range(count):
        e, c = lat // 2, lat % 2
        pairs.append((lat, e * 2 + 1 - c if along_core else (1 - e) * 2 + c))
    return pairs


def shards(
    images,
    lats,
    media,
    latents,
    counts,
    cotangent,
    attend_weight,
    output_weight,
    expand_weight,
    shrink_weight,
    layer_gains,
    layer_biases,
    attend_momentum,
    output_momentum,
    expand_momentum,
    shrink_momentum,
    gains_momentum,
    biases_momentum,
    attend_average,
    output_average,
    expand_average,
    shrink_average,
    gains_average,
    biases_average,
):
    devices = images * lats
    depth = images // 2
    fast = devices == BLOCKS and lats == 4 and images % 2 == 0
    samples, lat_dev, width = latents.shape
    rows = samples * lat_dev
    ff = expand_weight.shape[1]
    inner = attend_weight.shape[1] // 3
    patch_dev = media.shape[0]
    frames = patch_dev // PATCH_IMG
    over_core = functools.partial(lax.ppermute, axis_name="lat", perm=lat_pairs(lats, True))
    over_y = functools.partial(lax.ppermute, axis_name="lat", perm=lat_pairs(lats, False))

    attend_rows = attend_weight.shape[0]
    small = jnp.concatenate([layer_gains, layer_biases], axis=1)
    small = jnp.pad(small, ((0, 0), (0, LANES - small.shape[1])))
    attend_shard = jnp.concatenate([attend_weight, small], axis=1).astype(BF16)
    if fast:
        feed_shard = pack_feed(
            expand_weight.astype(BF16), shrink_weight.astype(BF16), output_weight.astype(BF16)
        )
        attend = gather_fast(attend_shard, depth, 1).reshape(width, attend_shard.shape[1])
        attend, feed_shard = lax.optimization_barrier((attend, feed_shard))
        feed = gather_fast(feed_shard, depth, 2)
    else:

        def everywhere(x):
            return lax.all_gather(x.astype(BF16), AXES, axis=0, tiled=True)

        attend = everywhere(attend_shard)
        feed = pack_feed(
            everywhere(expand_weight).reshape(BLOCKS, width // BLOCKS, ff),
            everywhere(shrink_weight).reshape(BLOCKS, ff // BLOCKS, width),
            everywhere(output_weight).reshape(BLOCKS, inner // BLOCKS, width),
        )
    gains = attend[:, 3 * inner : 3 * inner + 8].astype(F32).T

    sample_ends = jnp.cumsum(counts[0])
    first_frame = lax.axis_index("lat") * frames
    frame_ids = first_frame + jnp.arange(frames, dtype=jnp.int32)
    ids = jnp.sum((frame_ids[:, None] >= sample_ends[None, :]).astype(jnp.int32), axis=1)
    ids = jnp.clip(ids, 0, samples - 1)

    latent_flat = latents.reshape(rows, width)
    query, latent_key, latent_value = latent_project(latent_flat, gains, attend, inner)
    cut = (samples, lat_dev, inner)
    latent_key = latent_key.reshape(cut)
    latent_value = latent_value.reshape(cut)

    def to_group(own):
        other = over_y(own)
        return [own, over_core(own), other, over_core(other)]

    queries = to_group(query.reshape(cut))
    keys, values = media_project(media, gains, attend, inner)
    keep, send, keep_st, send_st = attention_forward(
        ids, queries, keys, values, latent_key, latent_value
    )
    got, got_st = over_core(send), over_core(send_st)
    flat_o, flat_s = (2, rows, inner), (2, rows, LANES)
    own, own_st, away, away_st = join_cores(
        keep.reshape(flat_o), keep_st.reshape(flat_s), got.reshape(flat_o), got_st.reshape(flat_s)
    )
    got, got_st = over_y(away), over_y(away_st)
    cot_flat = cotangent.reshape(rows, width)
    out_rows, mixed_grad, context_grad, tile, gain_f, grad_feed = feed_forward(
        own, own_st, got, got_st, latent_flat, cot_flat, gains, feed
    )
    grads = to_group(context_grad.reshape(cut))
    tiles = to_group(tile.reshape(samples, lat_dev, LANES))
    grad_media, latent_kv, keep, send, grad_kv, gain_m = attention_backward(
        ids,
        queries,
        grads,
        tiles,
        keys,
        values,
        latent_key,
        latent_value,
        media,
        gains,
        attend,
    )
    got = over_core(send)
    pair = keep.astype(F32) + got.astype(F32)
    got = over_y(pair[1].astype(BF16))
    latents_grad, grad_attend = latent_backward(
        latent_flat,
        mixed_grad,
        pair[0].reshape(rows, inner),
        got.reshape(rows, inner),
        latent_kv.reshape(rows, 2 * inner),
        gains,
        attend,
        grad_kv,
        gain_m,
        gain_f,
    )
    if fast:
        mine = scatter_fast(
            grad_attend.reshape(BLOCKS, attend_rows, grad_attend.shape[1]), depth, 3, 16
        )
        mine_feed = scatter_fast(grad_feed, depth, 4, 16)
        own_expand, own_shrink, own_output = unpack_feed(
            mine_feed, attend_rows, shrink_weight.shape[0]
        )
    else:

        def owners(x):
            return lax.psum_scatter(x.astype(F32), AXES, scatter_dimension=0, tiled=True)

        mine = owners(grad_attend)
        own_expand, own_shrink, own_output = unpack_feed(grad_feed, width // BLOCKS, ff // BLOCKS)
        own_expand = owners(own_expand.reshape(width, ff))
        own_shrink = owners(own_shrink.reshape(ff, width))
        own_output = owners(own_output.reshape(inner, width))
    small = mine[:, 3 * inner :]
    owned = (
        mine[:, : 3 * inner],
        own_output,
        own_expand,
        own_shrink,
        small[:, 0:3],
        small[:, 3:6],
    )
    squares = sum(jnp.sum(piece * piece) for piece in owned)
    if fast:
        squares = total_fast(jnp.full((8, LANES), squares, F32), images, lats, 5)[0, 0]
    else:
        squares = lax.psum(squares, AXES)
    grad_norm = jnp.sqrt(squares)
    factor = jnp.minimum(1.0, CLIP_NORM / (grad_norm + 1e-06))
    masters = (
        attend_weight,
        output_weight,
        expand_weight,
        shrink_weight,
        layer_gains,
        layer_biases,
    )
    moments = (
        attend_momentum,
        output_momentum,
        expand_momentum,
        shrink_momentum,
        gains_momentum,
        biases_momentum,
    )
    averages = (
        attend_average,
        output_average,
        expand_average,
        shrink_average,
        gains_average,
        biases_average,
    )
    decay_rates = (DECAY, DECAY, DECAY, DECAY, 0.0, 0.0)
    step_rate = step_size(width, inner, ff)
    new_masters = []
    new_buffers = []
    new_smoothed = []
    for master, moment, average, reduced, decay_rate, rate_scale in zip(
        masters, moments, averages, owned, decay_rates, RATE_SCALES
    ):
        step_grad = factor * reduced + decay_rate * master
        buffer = MOMENTUM * moment + step_grad
        master_new = master - step_rate * rate_scale * (step_grad + MOMENTUM * buffer)
        new_masters.append(master_new)
        new_buffers.append(buffer)
        new_smoothed.append(AVERAGING * average + (1.0 - AVERAGING) * master_new)
    return (
        out_rows.reshape(latents.shape),
        grad_media,
        latents_grad.reshape(latents.shape),
        grad_norm,
        *new_masters,
        *new_buffers,
        *new_smoothed,
    )


def solution(mesh):
    rows = P(AXES, None)
    split = P("img", "lat", None)
    return jax.shard_map(
        functools.partial(shards, mesh.shape["img"], mesh.shape["lat"]),
        mesh=mesh,
        in_specs=(rows, split, P("img", None), split) + (rows,) * 18,
        out_specs=(split, rows, split, P()) + (rows,) * 18,
        check_vma=False,
    )
```

time: 1610 us -> 490 us (0.30)
  waiting for transfers between devices: 958 us -> 18 us
  Pallas kernels: 0 us -> 416 us
  matrix products: 213 us -> 0 us
  blocking collectives: 141 us -> 0 us
  local copies, waits for them, and re-layouts: 142 us -> 16.7 us
  other arithmetic: 117 us -> 18.7 us
    reduce_scatter x6 -> x0, waiting for transfers between devices: 532 us -> none  [the longest x1 184 us: shards(): lax.psum_scatter(grad_shrink, ('img', 'lat'), scatter_dimension=0, tiled=...]
    pallas_call x0 -> x12, Pallas kernels: none -> 416 us  [the longest x2 134 us: scatter_fast(): pl.pallas_call(functools.partial(scatter_kernel, depth, chunk), out_shape...]
    unnamed x16 -> x0, waiting for transfers between devices: 260 us -> none
    dot_general x45 -> x0, matrix products: 190 us -> none  [the longest x5 54.9 us: matmul_right_t(): lax.dot_general(first_op, second_op, (((1,), (1,)), ((), ())), preferred_...]
    all_gather x6 -> x0, waiting for transfers between devices: 165 us -> none  [the longest x1 78.9 us: shards(): lax.all_gather(to_half(expand_weight), ('img', 'lat'), axis=0, tiled=True)]
    all_gather x5 -> x0, blocking collectives: 99.4 us -> none  [the longest x1 43.3 us: shards(): lax.all_gather(to_half(layer_biases), ('img', 'lat'), axis=0, tiled=True)]
    dynamic_slice x91 -> x0, local copies, waits for them, and re-layouts: 57.7 us -> none  [the longest x18 17.6 us: view(): window_query = lax.dynamic_slice_in_dim(queries, low_sample, width, 0)]
    psum x1 -> x0, blocking collectives: 41.7 us -> none  [shards(): grad_norm = jnp.sqrt(lax.psum(squares, ('img', 'lat')))]
  transfers between devices with their start and end apart: 14 -> 15, of which waited for: 10 -> 6; matrix products, arithmetic and copies ran while one was open for 20% -> 2% of each run, Pallas kernels for 0% -> 43%
where the time goes in v1:
time: 490 us; the launch traced here: 485 us
  Pallas kernels  416 us (85%)
  other arithmetic  18.7 us (4%)
  waiting for transfers between devices  18 us (4%)
  local copies, waits for them, and re-layouts  16.7 us (3%)
  starting transfers between devices  8.3 us (2%)
  between operations  7 us (1%)
    pallas_call x2, Pallas kernels, scatter_fast(): pl.pallas_call(functools.partial(scatter_kernel, depth, chunk), out_shape...  134 us
    pallas_call x2, Pallas kernels, gather_fast(): pl.pallas_call(functools.partial(gather_kernel, depth), out_shape=jax.Sha...  116 us
    pallas_call x1, Pallas kernels, attention_backward(): pl.pallas_call(backward_kernel, grid_spec=pltpu.PrefetchScalarGridSpec(nu...  52.3 us
    pallas_call x1, Pallas kernels, attention_forward(): pl.pallas_call(forward_kernel, grid_spec=pltpu.PrefetchScalarGridSpec(num...  35.9 us
    pallas_call x1, Pallas kernels, feed_forward(): pl.pallas_call(feed_kernel, out_shape=(jax.ShapeDtypeStruct((rows, width)...  34 us
    pallas_call x1, Pallas kernels, media_project(): pl.pallas_call(media_kernel, grid=(rows // PATCH_IMG,), out_shape=(out, o...  15.1 us
    ppermute x3, waiting for transfers between devices, to_group(): other = over_y(own)  13.1 us
    pallas_call x1, Pallas kernels, latent_backward(): pl.pallas_call(last_kernel, out_shape=(jax.ShapeDtypeStruct(latents.shape...  9.97 us
  transfers between devices with their start and end apart: 15, of which 6 were waited for; matrix products, arithmetic and copies ran while one was open for 2% of the time, Pallas kernels for 43%

profile of v1, /device:TPU:0, one launch (start us, length us, event | category | flops | bytes accessed | tf_op | source)
XLA Modules:
  0.0 484.8 jit_solution(9340138434608396639)
XLA Ops:
  3.1 27.6 %gather1.1 = bf16[32,32,1664]{2,1,0:T(8,128)(2,1)} custom-call(bf16[32,1664]{1,0:T(8,128)(2,1)} %fusion.2.x_ref), custom_call_target="tpu_custom_call" | custom-call | tf_op jit(solution)/shard_map/gather1/pallas_call | solution.py:182
  34.2 4.9 %latent_project.1 = (bf16[384,512]{1,0:T(8,128)(2,1)}, bf16[384,512]{1,0:T(8,128)(2,1)}, bf16[384,512]{1,0:T(8,128)(2,1)}) custom-call(f32[384,1024]{1,0:T(8,128)} %bitcast.43, f32[8,1024]{1,0:T(8,128)} %copy.165.gb_ref, bf16[1024,1664]{1,0:T(8,128)(2,1)} %bitcast.37), custom_call_target="tpu_custom_call" | custom-call | tf_op jit(solution)/shard_map/latent_project/pallas_call | solution.py:436
  40.1 15.1 %media_project.1 = (bf16[3072,512]{1,0:T(8,128)(2,1)}, bf16[3072,512]{1,0:T(8,128)(2,1)}) custom-call(bf16[3072,1024]{1,0:T(8,128)(2,1)} %m_ref.3, f32[8,1024]{1,0:T(8,128)} %copy.165.gb_ref, bf16[1024,1664]{1,0:T(8,128)(2,1)} %bitcast.38, bf16[1024,1664]{1,0:T(8,128)(2,1)} %bitcast.39), custom_call_target="tpu_custom_call" | custom-call | flops 6442450944 | bytes 12582912 | tf_op jit(solution)/shard_map/media_project/pallas_call | solution.py:406
  57.8 35.9 %attention_forward.1 = (bf16[2,24,16,512]{3,2,1,0:T(8,128)(2,1)}, bf16[2,24,16,512]{3,2,1,0:T(8,128)(2,1)}, f32[2,24,16,128]{3,2,1,0:T(8,128)}, f32[2,24,16,128]{3,2,1,0:T(8,128)}) custom-call(s32[12]{0:T(128)} %broadcast_clamp_fusion.ids, bf16[24,16,512]{2,1,0:T(8,128)(2,1)} %bitcast.52, bf16[24,16,512]{2,1,0:T(8,128)(2,1)} %copy-done.5, ...), custom_call_target="tpu_custom_call" | custom-call | tf_op jit(solution)/shard_map/attention_forward/pallas_call | solution.py:566
  94.3 2.5 collective-permute-done.4
  97.9 4.5 join_cores.1
  104.4 88.0 %gather2.1.w_ref = bf16[32,272,1024]{2,1,0:T(8,128)(2,1)} custom-call(bf16[272,1024]{1,0:T(8,128)(2,1)} %pad_maximum_fusion.x_ref), custom_call_target="tpu_custom_call" | custom-call | tf_op jit(solution)/shard_map/gather2/pallas_call | solution.py:182
  193.2 34.0 %feed_forward.1 = (f32[384,1024]{1,0:T(8,128)}, f32[384,1024]{1,0:T(8,128)}, bf16[384,512]{1,0:T(8,128)(2,1)}, f32[384,128]{1,0:T(8,128)}, f32[8,1024]{1,0:T(8,128)}, /*index=5*/bf16[32,272,1024]{2,1,0:T(8,128)(2,1)}) custom-call(f32[384,512]{1,0:T(8,128)} %get-tuple-element.61.own, f32[384,128]{1,0:T(8,128)} %get-tuple-element.62.own_st, ...), custom_call_target="tpu_custom_call" | custom-call | flops 20535312384 | bytes 35651584 | tf_op jit(solution)/shard_map/feed_forward/pallas_call | solution.py:787
  229.6 9.9 %collective-permute-done.8.g2 = bf16[24,16,512]{2,1,0:T(8,128)(2,1)S(1)} collective-permute-done((bf16[24,16,512]{2,1,0:T(8,128)(2,1)}, bf16[24,16,512]{2,1,0:T(8,128)(2,1)S(1)}, u32[]{:S(2)}, u32[]{:S(2)}) %collective-permute-start.8) | collective-permute-done | bytes 393248 | tf_op jit(solution)/shard_map/ppermute | solution.py:1132
  239.9 3.2 collective-permute-done.11.t2
  243.2 1.4 collective-permute-done.12.t3
  246.0 52.3 %attention_backward.1 = (bf16[3072,1024]{1,0:T(8,128)(2,1)}, bf16[24,16,1024]{2,1,0:T(8,128)(2,1)}, bf16[2,24,16,512]{3,2,1,0:T(8,128)(2,1)}, bf16[2,24,16,512]{...) custom-call(s32[12]{0:T(128)} %broadcast_clamp_fusion.ids, bf16[24,16,512]{2,1,0:T(8,128)(2,1)} %bitcast.53, ...), custom_call_target="tpu_custom_call" | custom-call | tf_op jit(solution)/shard_map/attention_backward/pallas_call | solution.py:934
  300.9 1.4 convert_add_fusion
  304.2 1.4 copy.182
  305.6 105.5 %scatter4.1 = f32[272,1024]{1,0:T(8,128)} custom-call(bf16[32,272,1024]{2,1,0:T(8,128)(2,1)} %get-tuple-element.79.g_ref), custom_call_target="tpu_custom_call" | custom-call | tf_op jit(solution)/shard_map/scatter4/pallas_call | solution.py:304
  411.1 1.5 multiply_reduce_fusion.3
  412.5 1.9 multiply_reduce_fusion
  416.2 10.0 %latent_backward.1 = (f32[384,1024]{1,0:T(8,128)}, bf16[1024,1664]{1,0:T(8,128)(2,1)}) custom-call(f32[384,1024]{1,0:T(8,128)} %bitcast.45, f32[384,1024]{1,0:T(8,128)} %get-tuple-element.70.mixed_grad, f32[384,512]{1,0:T(8,128)} %bitcast.47, bf16[384,512]{1,0:T(8,128)(2,1)} %bitcast.63, bf16[384,1024]{1,0:T(8,128)(2,1)} %bitcast.60, ...), custom_call_target="tpu_custom_call" | custom-call | tf_op jit(solution)/shard_map/latent_backward/pallas_call | solution.py:1008
  426.2 28.8 %scatter3.1 = f32[32,1664]{1,0:T(8,128)} custom-call(bf16[32,32,1664]{2,1,0:T(8,128)(2,1)} %bitcast.46), custom_call_target="tpu_custom_call" | custom-call | tf_op jit(solution)/shard_map/scatter3/pallas_call | solution.py:304
  455.0 1.6 multiply_reduce_fusion.2
  456.6 1.5 multiply_reduce_fusion.4
  462.6 9.5 %total5.1 = f32[8,128]{1,0:T(8,128)} custom-call(f32[8,128]{1,0:T(8,128)} %broadcast_in_dim.2.x_ref), custom_call_target="tpu_custom_call" | custom-call | tf_op jit(solution)/shard_map/total5/pallas_call | solution.py:366
  478.9 1.3 multiply_add_fusion
  482.2 1.3 multiply_add_fusion.1
  (145 shorter events, 32.8 us)
Async XLA Ops:
  39.1 16.2 %collective-permute-start.1 = (bf16[24,16,512]{2,1,0:T(8,128)(2,1)}, bf16[24,16,512]{2,1,0:T(8,128)(2,1)S(1)}, u32[]{:S(2)}, u32[]{:S(2)}) collective-permute-start(bf16[24,16,512]{2,1,0:T(8,128)(2,1)} %bitcast.50), channel_id=1, source_target_pairs={{0,2},{1,3},{2,0},{3,1},{4,6},{5,7},{6,4},{7,5},{8,10},{9,11},{10,... | collective-permute-start | bytes 1179656 | tf_op jit(solution)/shard_map/ppermute | solution.py:1132
  40.0 16.7 %collective-permute-start = (bf16[24,16,512]{2,1,0:T(8,128)(2,1)}, bf16[24,16,512]{2,1,0:T(8,128)(2,1)S(1)}, u32[]{:S(2)}, u32[]{:S(2)}) collective-permute-start(bf16[24,16,512]{2,1,0:T(8,128)(2,1)} %bitcast.51), channel_id=1, source_target_pairs={{0,1},{1,0},{2,3},{3,2},{4,5},{5,4},{6,7},{7,6},{8,9},{9,8},{10,11... | collective-permute-start | bytes 1179656 | tf_op jit(solution)/shard_map/ppermute | solution.py:1133
  55.3 1.8 collective-permute-start.2
  93.7 3.1 collective-permute-start.3
  94.1 2.7 collective-permute-start.4
  102.4 90.1 %collective-permute-start.5 = (bf16[384,512]{1,0:T(8,128)(2,1)}, bf16[384,512]{1,0:T(8,128)(2,1)S(1)}, u32[]{:S(2)}, u32[]{:S(2)}) collective-permute-start(bf16[384,512]{1,0:T(8,128)(2,1)} %get-tuple-element.63), channel_id=1, source_target_pairs={{0,2},{1,3},{2,0},{3,1},{4,6},{5,7},{6,4},{7,5},{8,10},{9,11},{10,... | collective-permute-start | bytes 1179656 | tf_op jit(solution)/shard_map/ppermute | solution.py:1145
  103.5 88.9 %collective-permute-start.6 = (f32[384,128]{1,0:T(8,128)}, f32[384,128]{1,0:T(8,128)S(1)}, u32[]{:S(2)}, u32[]{:S(2)}) collective-permute-start(f32[384,128]{1,0:T(8,128)} %get-tuple-element.64), channel_id=1, source_target_pairs={{0,2},{1,3},{2,0},{3,1},{4,6},{5,7},{6,4},{7,5},{8,10},{9,11},{10,... | collective-permute-start | bytes 589832 | tf_op jit(solution)/shard_map/ppermute | solution.py:1145
  227.2 12.2 %collective-permute-start.8 = (bf16[24,16,512]{2,1,0:T(8,128)(2,1)}, bf16[24,16,512]{2,1,0:T(8,128)(2,1)S(1)}, u32[]{:S(2)}, u32[]{:S(2)}) collective-permute-start(bf16[24,16,512]{2,1,0:T(8,128)(2,1)} %bitcast.66), channel_id=1, source_target_pairs={{0,2},{1,3},{2,0},{3,1},{4,6},{5,7},{6,4},{7,5},{8,10},{9,11},{10,... | collective-permute-start | bytes 1179656 | tf_op jit(solution)/shard_map/ppermute | solution.py:1132
  228.4 14.8 %collective-permute-start.7 = (bf16[24,16,512]{2,1,0:T(8,128)(2,1)}, bf16[24,16,512]{2,1,0:T(8,128)(2,1)S(1)}, u32[]{:S(2)}, u32[]{:S(2)}) collective-permute-start(bf16[24,16,512]{2,1,0:T(8,128)(2,1)} %bitcast.67), channel_id=1, source_target_pairs={{0,1},{1,0},{2,3},{3,2},{4,5},{5,4},{6,7},{7,6},{8,9},{9,8},{10,11... | collective-permute-start | bytes 1179656 | tf_op jit(solution)/shard_map/ppermute | solution.py:1133
  228.6 70.0 %copy-start.29 = (f32[32,3]{0,1:T(4,128)S(1)}, f32[32,3]{0,1:T(4,128)}, u32[]{:S(2)}) copy-start(f32[32,3]{0,1:T(4,128)} %param.30) | copy-start | bytes 1156
  228.6 70.0 %copy-start.30 = (f32[32,3]{0,1:T(4,128)S(1)}, f32[32,3]{0,1:T(4,128)}, u32[]{:S(2)}) copy-start(f32[32,3]{0,1:T(4,128)} %param.31) | copy-start | bytes 1156
  228.6 70.3 %copy-start.31 = (f32[32,3]{0,1:T(4,128)S(1)}, f32[32,3]{0,1:T(4,128)}, u32[]{:S(2)}) copy-start(f32[32,3]{0,1:T(4,128)} %param.36) | copy-start | bytes 1156
  228.6 70.4 %copy-start.32 = (f32[32,3]{0,1:T(4,128)S(1)}, f32[32,3]{0,1:T(4,128)}, u32[]{:S(2)}) copy-start(f32[32,3]{0,1:T(4,128)} %param.37) | copy-start | bytes 1156
  228.6 71.1 %copy-start.33 = (f32[32,3]{0,1:T(4,128)S(1)}, f32[32,3]{0,1:T(4,128)}, u32[]{:S(2)}) copy-start(f32[32,3]{0,1:T(4,128)} %param.42) | copy-start | bytes 1156
  228.6 14.6 %collective-permute-start.11 = (f32[24,16,128]{2,1,0:T(8,128)}, f32[24,16,128]{2,1,0:T(8,128)S(1)}, u32[]{:S(2)}, u32[]{:S(2)}) collective-permute-start(f32[24,16,128]{2,1,0:T(8,128)} %bitcast.69), channel_id=1, source_target_pairs={{0,2},{1,3},{2,0},{3,1},{4,6},{5,7},{6,4},{7,5},{8,10},{9,11},{10,... | collective-permute-start | bytes 589832 | tf_op jit(solution)/shard_map/ppermute | solution.py:1132
  239.4 5.2 %collective-permute-start.9 = (bf16[24,16,512]{2,1,0:T(8,128)(2,1)S(1)}, bf16[24,16,512]{2,1,0:T(8,128)(2,1)S(1)}, u32[]{:S(2)}, u32[]{:S(2)}) collective-permute-start(bf16[24,16,512]{2,1,0:T(8,128)(2,1)S(1)} %collective-permute-done.8.g2), channel_id=1, source_target_pairs={{0,1},{1,0},{2,3},{3,2},{4,5},{5,4},{6,7},{7,6},{8,9},{9,8},{10,11... | collective-permute-start | bytes 1179656 | tf_op jit(solution)/shard_map/ppermute | solution.py:1133
  239.4 3.8 collective-permute-start.10
  243.2 1.4 collective-permute-start.12
  298.3 2.6 collective-permute-start.13
  302.4 113.0 %collective-permute-start.14 = (bf16[24,16,512]{2,1,0:T(8,128)(2,1)S(1)}, bf16[24,16,512]{2,1,0:T(8,128)(2,1)S(1)}, u32[]{:S(2)}, u32[]{:S(2)}) collective-permute-start(bf16[24,16,512]{2,1,0:T(8,128)(2,1)S(1)} %fusion), channel_id=1, source_target_pairs={{0,2},{1,3},{2,0},{3,1},{4,6},{5,7},{6,4},{7,5},{8,10},{9,11},{10,... | collective-permute-start | bytes 1179656 | tf_op jit(solution)/shard_map/ppermute | solution.py:1167
  426.1 47.9 %copy-start.26 = (f32[32,3]{1,0:T(8,128)S(1)}, f32[32,3]{1,0:T(8,128)}, u32[]{:S(2)}) copy-start(f32[32,3]{1,0:T(8,128)} %copy.182) | copy-start | bytes 1156
  426.2 52.6 %copy-start = (f32[272,1024]{1,0:T(8,128)S(1)}, f32[272,1024]{1,0:T(8,128)}, u32[]{:S(2)}) copy-start(f32[272,1024]{1,0:T(8,128)} %scatter4.1) | copy-start | bytes 3342340
  426.2 52.6 %copy-start.9 = (f32[128,1024]{1,0:T(8,128)S(1)}, f32[128,1024]{1,0:T(8,128)}, u32[]{:S(2)}) copy-start(f32[128,1024]{1,0:T(8,128)} %param.41) | copy-start | bytes 1572868
  426.2 52.6 %copy-start.10 = (f32[128,1024]{1,0:T(8,128)S(1)}, f32[128,1024]{1,0:T(8,128)}, u32[]{:S(2)}) copy-start(f32[128,1024]{1,0:T(8,128)} %param.35) | copy-start | bytes 1572868
  (29 other events, 201.5 us)

commit v2 on v1

--- a/solution.py
+++ b/solution.py
@@ -22,9 +22,28 @@
 LANES = 128
 BLOCKS = 32
 SCALE = HDIM ** (-0.5)
+MASKED = -1e30
 F32 = jnp.float32
 BF16 = jnp.bfloat16
 MESH = pl.DeviceIdType.MESH
+FRONT_PLAN = (
+    (6, "a1 z2 b0"),
+    (14, "z3"),
+    (16, "c0 b1 a2"),
+    (22, "c1 b2 a3"),
+    (24, "c2 b3 c3"),
+)
+BACK_PLAN = (
+    (0, "a0"),
+    (1, "a1"),
+    (2, "a2"),
+    (3, "a3"),
+    (5, "b0"),
+    (7, "c0 b1"),
+    (10, "c1 b2"),
+    (12, "c2"),
+    (13, "b3 c3"),
+)
 VMEM_LIMIT = 60 * 1024 * 1024
 
 
@@ -619,6 +638,424 @@
         compiler_params=params(),
         name="join_cores",
     )(keep, keep_st, got, got_st)
+
+
+class Gather:
+    def __init__(self, depth, x_ref, o_ref, local_sem, send_sem, recv_sem):
+        self.depth = depth
+        self.refs = x_ref, o_ref
+        self.sems = local_sem, send_sem, recv_sem
+        self.at = place()
+        one = first_partner(*self.at)
+        two = second_partner(*self.at)
+        self.homes = [self.at, one, two, second_partner(*one)]
+        self.order = z_order(depth)
+
+    def row(self, k, j):
+        a, _, _, c = self.at
+        _, b, e, _ = self.homes[j % 4]
+        return flat((a - k) % self.depth, b, e, c if j < 4 else 1 - c)
+
+    def copy(self, k, j):
+        x_ref, o_ref = self.refs
+        a, b, e, c = self.at
+        base = {1: 0, 2: 0, 3: 1}.get(j, j - 4)
+        if j == 0:
+            target, row, src = ((a + k) % self.depth, b, e, c), flat(a, b, e, c), x_ref
+        else:
+            target = self.homes[1] if j == 1 else self.homes[2] if j < 4 else (a, b, e, 1 - c)
+            row = self.row(k, base)
+            src = x_ref if (k, base) == (0, 0) else o_ref.at[row]
+        slot = k * 8 + j
+        return pltpu.make_async_remote_copy(
+            src_ref=src,
+            dst_ref=o_ref.at[row],
+            send_sem=self.sems[1].at[slot],
+            recv_sem=self.sems[2].at[slot],
+            device_id=device(*target),
+            device_id_type=MESH,
+        )
+
+    def arrive(self, k, j):
+        x_ref, o_ref = self.refs
+        a, b, e, c = self.at
+        slot = k * 8 + j
+        pltpu.make_async_remote_copy(
+            src_ref=x_ref,
+            dst_ref=o_ref.at[self.row(k, j)],
+            send_sem=self.sems[1].at[slot],
+            recv_sem=self.sems[2].at[slot],
+            device_id=device(a, b, e, 1 - c),
+            device_id_type=MESH,
+        ).wait_recv()
+
+    def own(self):
+        x_ref, o_ref = self.refs
+        return pltpu.make_async_copy(x_ref, o_ref.at[flat(*self.at)], self.sems[0])
+
+    def far(self, k):
+        self.copy(k, 0).start()
+
+    def begin(self):
+        self.own().start()
+        self.far(self.order[1])
+        self.first(0)
+
+    def first(self, k):
+        if k:
+            self.arrive(k, 0)
+        for j in (1, 2, 4):
+            self.copy(k, j).start()
+
+    def second(self, k):
+        self.arrive(k, 1)
+        self.copy(k, 3).start()
+        self.copy(k, 5).start()
+        self.arrive(k, 2)
+        self.copy(k, 6).start()
+
+    def third(self, k):
+        self.arrive(k, 3)
+        self.copy(k, 7).start()
+
+    def run(self, names):
+        acts = {"z": self.far, "a": self.first, "b": self.second, "c": self.third}
+        for name in names.split():
+            acts[name[0]](self.order[int(name[1:])])
+
+    def finish(self):
+        for k in range(self.depth):
+            for j in range(4, 8):
+                self.arrive(k, j)
+        for k in range(self.depth):
+            for j in range(8):
+                if k or j:
+                    self.copy(k, j).wait_send()
+        self.own().wait()
+
+
+def latent_mask(rows, inner):
+    row = lax.broadcasted_iota(jnp.int32, (HEADS * rows, inner), 0) // rows
+    col = lax.broadcasted_iota(jnp.int32, (HEADS * rows, inner), 1) // HDIM
+    return (row == col).astype(F32)
+
+
+def latent_attention(queries, keys, values, mask):
+    rows = keys.shape[0]
+    count = queries.shape[0]
+    half = mask.astype(BF16)
+    wide_k = jnp.concatenate([keys] * HEADS, axis=0) * half
+    wide_v = jnp.concatenate([values] * HEADS, axis=0) * half
+    scores = mm_nt(wide_k, queries).reshape(HEADS, rows, count)
+    top = jnp.max(scores, axis=1, keepdims=True)
+    probs = jnp.exp(scores - top)
+    total = jnp.sum(probs, axis=1)
+    out = mm_tn(probs.reshape(HEADS * rows, count).astype(BF16), wide_v)
+    zeros = jnp.zeros((LANES - HEADS, count), F32)
+
+    def tile(x):
+        return jnp.concatenate([x, zeros], axis=0).T
+
+    return out, tile(top.reshape(HEADS, count)), tile(total)
+
+
+def remote_copy(src, dst, sems, slot, target):
+    return pltpu.make_async_remote_copy(
+        src_ref=src,
+        dst_ref=dst,
+        send_sem=sems[0].at[slot],
+        recv_sem=sems[1].at[slot],
+        device_id=device(*target),
+        device_id_type=MESH,
+    )
+
+
+def front_kernel(
+    depth,
+    frames,
+    plan,
+    ids,
+    last,
+    has,
+    same,
+    shard_ref,
+    m_ref,
+    lat_ref,
+    gb_ref,
+    wq_ref,
+    feed_ref,
+    k_ref,
+    v_ref,
+    q_ref,
+    kl_ref,
+    vl_ref,
+    own,
+    own_st,
+    got,
+    got_st,
+    all_k,
+    all_v,
+    all_q,
+    outs,
+    tops,
+    sums,
+    keep,
+    keep_st,
+    send,
+    send_st,
+    core_o,
+    core_st,
+    away,
+    away_st,
+    y_o,
+    y_st,
+    local_sem,
+    send_sem,
+    recv_sem,
+    link_send,
+    link_recv,
+    out_sem,
+):
+    step = pl.program_id(0)
+    a, b, e, c = place()
+    twin, other = (a, b, e, 1 - c), (a, b, 1 - e, c)
+    links = link_send, link_recv
+    gather = Gather(depth, shard_ref, feed_ref, local_sem, send_sem, recv_sem)
+    clips, rows, inner = kl_ref.shape
+    groups = inner // (GROUP * HDIM)
+    width = GROUP * HDIM
+    mask = head_mask(F32)
+    mask_half = mask.astype(BF16)
+    query_copies = [
+        remote_copy(all_q.at[0], all_q.at[2], links, 0, other),
+        remote_copy(all_q.at[0], all_q.at[1], links, 1, twin),
+        remote_copy(all_q.at[2], all_q.at[3], links, 2, twin),
+    ]
+    core_copies = [
+        remote_copy(send, core_o, links, 3, twin),
+        remote_copy(send_st, core_st, links, 4, twin),
+    ]
+    y_copies = [
+        remote_copy(away, y_o, links, 5, other),
+        remote_copy(away_st, y_st, links, 6, other),
+    ]
+    keep_queries = pltpu.make_async_copy(all_q, q_ref, out_sem)
+
+    def clip_queries(clip):
+        return jnp.concatenate([all_q[r, clip] for r in range(4)], axis=0) * BF16(SCALE)
+
+    @pl.when(step == 0)
+    def _():
+        greet(depth, a, b, e, c)
+        hat, _ = normalise(lat_ref[...])
+        normed = (hat * gb_ref[1:2, :] + gb_ref[4:5, :]).astype(BF16)
+        all_q[0] = mm(normed, wq_ref[:, :inner]).astype(BF16).reshape(clips, rows, inner)
+        query_copies[0].start()
+        query_copies[1].start()
+        gather.begin()
+        kl_ref[...] = (
+            mm(normed, wq_ref[:, inner : 2 * inner]).astype(BF16).reshape(clips, rows, inner)
+        )
+        vl_ref[...] = (
+            mm(normed, wq_ref[:, 2 * inner : 3 * inner]).astype(BF16).reshape(clips, rows, inner)
+        )
+        outs[0] = jnp.zeros_like(outs[0])
+        tops[0] = jnp.zeros_like(tops[0])
+        sums[0] = jnp.zeros_like(sums[0])
+
+    @pl.when(step < frames)
+    def _():
+        hat, _ = normalise(m_ref[...].astype(F32))
+        normed = (hat * gb_ref[0:1, :] + gb_ref[3:4, :]).astype(BF16)
+        new_k = mm(normed, wq_ref[:, inner : 2 * inner]).astype(BF16)
+        new_v = mm(normed, wq_ref[:, 2 * inner : 3 * inner]).astype(BF16)
+        k_ref[...] = new_k
+        v_ref[...] = new_v
+        all_k[step] = new_k
+        all_v[step] = new_v
+
+    for when, names in plan[:-1]:
+
+        @pl.when(step == when)
+        def _(names=names):
+            gather.run(names)
+
+    @pl.when(step == frames // 2)
+    def _():
+        query_copies[0].wait()
+        query_copies[2].start()
+
+    @pl.when(step == frames)
+    def _():
+        query_copies[1].wait()
+        query_copies[2].wait()
+        keep_queries.start()
+
+    @pl.when((step >= frames) & (step < 2 * frames))
+    def _():
+        frame = step - frames
+        before = jnp.maximum(frame - 1, 0)
+        queries = clip_queries(ids[frame])
+        joined = same[frame] == 1
+        old_tops = jnp.where(joined, tops[before], MASKED)
+        old_sums = jnp.where(joined, sums[before], 0.0)
+        new_tops, new_sums = [], []
+        for g in range(groups):
+            cols = slice(g * width, (g + 1) * width)
+
+            def column(tile):
+                at = g * GROUP
+                return jnp.concatenate([tile[:, at + h : at + h + 1] for h in range(GROUP)], axis=0)
+
+            scores = mm_nt(spread_heads(queries, g, mask_half), all_k[frame, :, cols])
+            old_top = column(old_tops)
+            top = jnp.maximum(jnp.max(scores, axis=-1, keepdims=True), old_top)
+            probs = jnp.exp(scores - top)
+            shrink = jnp.exp(old_top - top)
+            total = jnp.sum(probs, axis=-1, keepdims=True) + column(old_sums) * shrink
+            part = take_heads(mm(probs.astype(BF16), all_v[frame, :, cols]), mask)
+            old = jnp.where(joined, outs[before, :, cols], 0.0)
+            outs[frame, :, cols] = part + old * take_heads(shrink, mask)
+            for h in range(GROUP):
+                new_tops.append(top[h * HDIM : (h + 1) * HDIM])
+                new_sums.append(total[h * HDIM : (h + 1) * HDIM])
+        tops[frame] = pack_columns(new_tops)
+        sums[frame] = pack_columns(new_sums)
+
+    @pl.when(step == 2 * frames)
+    def _():
+        wide = latent_mask(rows, inner)
+        lane = lax.broadcasted_iota(jnp.int32, (4 * rows, LANES), 1)
+
+        @pl.loop(0, clips)
+        def _(clip):
+            out, top, total = latent_attention(clip_queries(clip), kl_ref[clip], vl_ref[clip], wide)
+            at = last[clip]
+            there = has[clip] == 1
+            far_top = jnp.where(there, tops[at], MASKED)
+            far_sum = jnp.where(there, sums[at], 0.0)
+            far_out = jnp.where(there, outs[at], 0.0)
+            both = jnp.maximum(top, far_top)
+            near, far = jnp.exp(top - both), jnp.exp(far_top - both)
+            total = jnp.where(lane < HEADS, total * near + far_sum * far, 1.0)
+            stat = both + jnp.log(total)
+            out = out * expand_columns(near / total, inner)
+            out = out + far_out * expand_columns(far / total, inner)
+            for r in range(4):
+                part = slice(r * rows, (r + 1) * rows)
+                if r % 2:
+                    send[r // 2, clip] = out[part].astype(BF16)
+                    send_st[r // 2, clip] = stat[part]
+                else:
+                    keep[r // 2, clip] = out[part]
+                    keep_st[r // 2, clip] = stat[part]
+
+        for copy in core_copies:
+            copy.start()
+        for copy in core_copies:
+            copy.wait()
+
+        def flat_o(ref, n):
+            return ref[n].reshape(clips * rows, inner)
+
+        def flat_s(ref, n):
+            return ref[n].reshape(clips * rows, LANES)
+
+        out, stat = join_partials(
+            flat_o(keep, 1), flat_s(keep_st, 1), flat_o(core_o, 1), flat_s(core_st, 1)
+        )
+        away[...] = out.astype(BF16)
+        away_st[...] = stat
+        for copy in y_copies:
+            copy.start()
+        out, stat = join_partials(
+            flat_o(keep, 0), flat_s(keep_st, 0), flat_o(core_o, 0), flat_s(core_st, 0)
+        )
+        own[...] = out
+        own_st[...] = stat
+        gather.run(plan[-1][1])
+        for copy in y_copies:
+            copy.wait()
+        got[...] = y_o[...]
+        got_st[...] = y_st[...]
+        keep_queries.wait()
+        gather.finish()
+
+
+def front(ids, last, has, same, shard, media, latents, gains, attend, clips, inner, depth, plan):
+    rows = latents.shape[0] // clips
+    frames = media.shape[0] // PATCH_IMG
+    width = media.shape[1]
+    total = clips * rows
+    cut = (clips, rows, inner)
+
+    def whole(shape):
+        return pl.BlockSpec(shape, lambda i: (0,) * len(shape))
+
+    def block(columns):
+        return pl.BlockSpec((PATCH_IMG, columns), lambda i: (jnp.minimum(i, frames - 1), 0))
+
+    smem = pl.BlockSpec(memory_space=pltpu.SMEM)
+    kv = jax.ShapeDtypeStruct((media.shape[0], inner), BF16)
+    small = jax.ShapeDtypeStruct(cut, BF16)
+    stat = jax.ShapeDtypeStruct((total, LANES), F32)
+    count = depth * 8
+    return pl.pallas_call(
+        functools.partial(front_kernel, depth, frames, plan),
+        grid=(2 * frames + 1,),
+        out_shape=(
+            jax.ShapeDtypeStruct((count,) + shard.shape, BF16),
+            kv,
+            kv,
+            jax.ShapeDtypeStruct((4,) + cut, BF16),
+            small,
+            small,
+            jax.ShapeDtypeStruct((total, inner), F32),
+            stat,
+            jax.ShapeDtypeStruct((total, inner), BF16),
+            stat,
+        ),
+        in_specs=[smem] * 4
+        + [any_spec(), block(width), whole(latents.shape), whole(gains.shape), whole(attend.shape)],
+        out_specs=(
+            any_spec(),
+            block(inner),
+            block(inner),
+            any_spec(),
+            whole(cut),
+            whole(cut),
+            whole((total, inner)),
+            whole(stat.shape),
+            whole((total, inner)),
+            whole(stat.shape),
+        ),
+        scratch_shapes=[
+            pltpu.VMEM((frames, PATCH_IMG, inner), BF16),
+            pltpu.VMEM((frames, PATCH_IMG, inner), BF16),
+            pltpu.VMEM((4,) + cut, BF16),
+            pltpu.VMEM((frames, 4 * rows, inner), F32),
+            pltpu.VMEM((frames, 4 * rows, LANES), F32),
+            pltpu.VMEM((frames, 4 * rows, LANES), F32),
+            pltpu.VMEM((2,) + cut, F32),
+            pltpu.VMEM((2, clips, rows, LANES), F32),
+            pltpu.VMEM((2,) + cut, BF16),
+            pltpu.VMEM((2, clips, rows, LANES), F32),
+            pltpu.VMEM((2,) + cut, BF16),
+            pltpu.VMEM((2, clips, rows, LANES), F32),
+            pltpu.VMEM((total, inner), BF16),
+            pltpu.VMEM((total, LANES), F32),
+            pltpu.VMEM((total, inner), BF16),
+            pltpu.VMEM((total, LANES), F32),
+            pltpu.SemaphoreType.DMA,
+            pltpu.SemaphoreType.DMA((count,)),
+            pltpu.SemaphoreType.DMA((count,)),
+            pltpu.SemaphoreType.DMA((7,)),
+            pltpu.SemaphoreType.DMA((7,)),
+            pltpu.SemaphoreType.DMA,
+        ],
+        compiler_params=params(collective_id=2, has_side_effects=True),
+        name="front",
+    )(ids, last, has, same, shard, media, latents, gains, attend)
 
 
 def feed_kernel(
@@ -1018,6 +1455,468 @@
     )(latents, mixed_grad, first, second, grad_kv, gains, attend, grad_w, gain_m, gain_f)
 
 
+class Scatter:
+    def __init__(self, depth, chunk, g_ref, buffers, load_sem, sems):
+        self.depth = depth
+        self.chunk = chunk
+        self.g_ref = g_ref
+        self.own, self.from_c, self.from_two, self.from_one, self.from_z = buffers
+        self.load_sem = load_sem
+        self.sems = sems
+        self.at = place()
+        self.one = first_partner(*self.at)
+        self.two = second_partner(*self.at)
+        self.homes = [self.at, self.one, self.two, second_partner(*self.one)]
+        a, b, e, c = self.at
+        self.twin = (a, b, e, 1 - c)
+        order = z_order(depth)
+        self.order = order[1:] + order[:1]
+        self.rows = self.own.shape[1]
+
+    def row(self, k, j, core):
+        _, b, e, _ = self.homes[j]
+        return flat((self.at[0] + k) % self.depth, b, e, core)
+
+    def load(self, k, j):
+        slot = k * 4 + j
+        src = self.g_ref.at[self.row(k, j, self.at[3])]
+        return pltpu.make_async_copy(src, self.own.at[slot], self.load_sem.at[slot])
+
+    def to_twin(self, k, j):
+        src = self.g_ref.at[self.row(k, (0, 2, 1, 3)[j], 1 - self.at[3])]
+        return remote_copy(src, self.from_c.at[k * 4 + j], self.sems, k * 8 + j, self.twin)
+
+    def to_two(self, k, j):
+        spot = self.from_two.at[k * 2 + j - 2]
+        return remote_copy(self.own.at[k * 4 + j], spot, self.sems, k * 8 + 2 + j, self.two)
+
+    def to_one(self, k):
+        return remote_copy(
+            self.own.at[k * 4 + 1], self.from_one.at[k], self.sems, k * 8 + 6, self.one
+        )
+
+    def to_far(self, k):
+        a, b, e, c = self.at
+        target = ((a + k) % self.depth, b, e, c)
+        return remote_copy(
+            self.own.at[k * 4], self.from_z.at[k - 1], self.sems, k * 8 + 7, target
+        )
+
+    def add(self, slot, spot):
+        mine = self.own.at[slot]
+        add_into(mine, mine, spot, self.rows, self.chunk)
+
+    def begin(self):
+        for k in self.order:
+            for j in (3, 2, 1, 0):
+                self.load(k, j).start()
+                self.to_twin(k, j).start()
+
+    def first(self, k):
+        for j in (3, 2, 1, 0):
+            self.load(k, j).wait()
+            self.to_twin(k, j).wait_recv()
+            self.add(k * 4 + j, self.from_c.at[k * 4 + j])
+            if j >= 2:
+                self.to_two(k, j).start()
+
+    def second(self, k):
+        for j in (3, 2):
+            self.to_two(k, j).wait_recv()
+            self.add(k * 4 + j - 2, self.from_two.at[k * 2 + j - 2])
+            if j == 3:
+                self.to_one(k).start()
+
+    def third(self, k):
+        self.to_one(k).wait_recv()
+        self.add(k * 4, self.from_one.at[k])
+        if k:
+            self.to_far(k).start()
+
+    def run(self, names):
+        acts = {"a": self.first, "b": self.second, "c": self.third}
+        for name in names.split():
+            acts[name[0]](self.order[int(name[1:])])
+
+    def finish(self, o_ref):
+        for k in range(1, self.depth):
+            self.to_far(k).wait_recv()
+
+        @pl.loop(0, self.rows // self.chunk)
+        def _(step):
+            part = pl.ds(step * self.chunk, self.chunk)
+            total = self.own[0, part, :].astype(F32)
+            for k in range(1, self.depth):
+                total = total + self.from_z[k - 1, part, :].astype(F32)
+            o_ref[part, :] = total
+
+        for k in range(self.depth):
+            for j in range(4):
+                self.to_twin(k, j).wait_send()
+            self.to_two(k, 3).wait_send()
+            self.to_two(k, 2).wait_send()
+            self.to_one(k).wait_send()
+            if k:
+                self.to_far(k).wait_send()
+
+
+def scatter_buffers(depth, rows, cols):
+    def slots(n):
+        return pltpu.VMEM((n, rows, cols), BF16)
+
+    return [slots(depth * 4), slots(depth * 4), slots(depth * 2), slots(depth), slots(depth - 1)]
+
+
+def scatter_sems(depth):
+    return [
+        pltpu.SemaphoreType.DMA((depth * 4,)),
+        pltpu.SemaphoreType.DMA((depth * 8,)),
+        pltpu.SemaphoreType.DMA((depth * 8,)),
+    ]
+
+
+def latent_attention_back(queries, grads, stats, keys, values, mask):
+    rows = keys.shape[0]
+    count = queries.shape[0]
+    half = mask.astype(BF16)
+    wide_k = jnp.concatenate([keys] * HEADS, axis=0) * half
+    wide_v = jnp.concatenate([values] * HEADS, axis=0) * half
+    cut = (HEADS, rows, count)
+    scores = mm_nt(wide_k, queries).reshape(cut)
+    probs = jnp.exp(scores - stats[:HEADS][:, None, :])
+    grad_probs = mm_nt(wide_v, grads).reshape(cut)
+    grad_scores = probs * (grad_probs - stats[HEADS : 2 * HEADS][:, None, :])
+    grad_scores = grad_scores.reshape(HEADS * rows, count).astype(BF16)
+    probs = probs.reshape(HEADS * rows, count).astype(BF16)
+
+    def fold(full):
+        full = full * mask
+        total = full[:rows]
+        for h in range(1, HEADS):
+            total = total + full[h * rows : (h + 1) * rows]
+        return total
+
+    grad_kv = [fold(mm(grad_scores, queries)), fold(mm(probs, grads))]
+    return mm_tn(grad_scores, wide_k), jnp.concatenate(grad_kv, axis=1).astype(BF16)
+
+
+def to_lines(tile):
+    return tile.T[: 2 * HEADS]
+
+
+def from_lines(lines):
+    zeros = jnp.zeros((LANES - lines.shape[0], lines.shape[1]), F32)
+    return jnp.concatenate([lines, zeros], axis=0).T
+
+
+def back_kernel(
+    depth,
+    frames,
+    chunk,
+    plan,
+    ids,
+    last,
+    has,
+    same,
+    g_ref,
+    q_ref,
+    context_grad,
+    tile_ref,
+    k_ref,
+    v_ref,
+    m_ref,
+    kl_ref,
+    vl_ref,
+    gb_ref,
+    w_ref,
+    lat_ref,
+    mixed_ref,
+    gain_f,
+    media_grad,
+    latents_grad,
+    pack_ref,
+    mine_ref,
+    own,
+    from_c,
+    from_two,
+    from_one,
+    from_z,
+    load_sem,
+    send_sem,
+    recv_sem,
+    all_g,
+    lines,
+    tiles,
+    weight_acc,
+    gain_acc,
+    outs,
+    latent_kv,
+    keep,
+    send,
+    core_q,
+    away,
+    y_q,
+    link_send,
+    link_recv,
+    mixed_sem,
+):
+    step = pl.program_id(0)
+    a, b, e, c = place()
+    twin, other = (a, b, e, 1 - c), (a, b, 1 - e, c)
+    links = link_send, link_recv
+    scatter = Scatter(
+        depth, chunk, g_ref, (own, from_c, from_two, from_one, from_z), load_sem, (send_sem, recv_sem)
+    )
+    clips, rows, inner = kl_ref.shape
+    total_rows = clips * rows
+    groups = inner // (GROUP * HDIM)
+    width = GROUP * HDIM
+    mask = head_mask(F32)
+    mask_half = mask.astype(BF16)
+    grad_copies = [
+        remote_copy(all_g.at[0], all_g.at[2], links, 0, other),
+        remote_copy(all_g.at[0], all_g.at[1], links, 1, twin),
+        remote_copy(all_g.at[2], all_g.at[3], links, 2, twin),
+    ]
+    line_copies = [
+        remote_copy(lines.at[0], lines.at[2], links, 3, other),
+        remote_copy(lines.at[0], lines.at[1], links, 4, twin),
+        remote_copy(lines.at[2], lines.at[3], links, 5, twin),
+    ]
+    core_copy = remote_copy(send, core_q, links, 6, twin)
+    y_copy = remote_copy(away, y_q, links, 7, other)
+
+    def clip_queries(clip):
+        return jnp.concatenate([q_ref[r, clip] for r in range(4)], axis=0) * BF16(SCALE)
+
+    def clip_grads(clip):
+        return jnp.concatenate([all_g[r, clip] for r in range(4)], axis=0)
+
+    def clip_stats(clip):
+        return jnp.concatenate([tiles[r, clip] for r in range(4)], axis=0).T
+
+    @pl.when(step == 0)
+    def _():
+        all_g[0] = context_grad[...]
+        lines[0] = to_lines(tile_ref[...])
+        greet(depth, a, b, e, c)
+        for copies in (grad_copies, line_copies):
+            copies[0].start()
+            copies[1].start()
+        scatter.begin()
+        gain_acc[...] = jnp.zeros_like(gain_acc)
+        weight_acc[...] = jnp.zeros_like(weight_acc)
+        outs[0] = jnp.zeros_like(outs[0])
+
+    for when, names in plan[:-1]:
+
+        @pl.when(step == when)
+        def _(names=names):
+            scatter.run(names)
+
+    @pl.when(step == 0)
+    def _():
+        for copies in (grad_copies, line_copies):
+            copies[0].wait()
+            copies[2].start()
+        for copies in (grad_copies, line_copies):
+            copies[1].wait()
+            copies[2].wait()
+        for r in range(4):
+            tiles[r] = from_lines(lines[r]).reshape(clips, rows, LANES)
+
+    @pl.when((step >= 1) & (step <= frames))
+    def _():
+        frame = step - 1
+        before = jnp.maximum(frame - 1, 0)
+        clip = ids[frame]
+        joined = same[frame] == 1
+        queries, grads, stats = clip_queries(clip), clip_grads(clip), clip_stats(clip)
+        key_parts, value_parts = [], []
+        for g in range(groups):
+            cols = slice(g * width, (g + 1) * width)
+
+            def line(first):
+                at = first + g * GROUP
+                return jnp.concatenate([stats[at + h : at + h + 1, :] for h in range(GROUP)], axis=1)
+
+            wide_q = spread_heads(queries, g, mask_half)
+            wide_g = spread_heads(grads, g, mask_half)
+            keys = k_ref[:, cols]
+            probs = jnp.exp(mm_nt(keys, wide_q) - line(0))
+            grad_probs = mm_nt(v_ref[:, cols], wide_g)
+            grad_scores = (probs * (grad_probs - line(HEADS))).astype(BF16)
+            key_parts.append(mm(grad_scores, wide_q))
+            value_parts.append(mm(probs.astype(BF16), wide_g))
+            part = take_heads(mm_tn(grad_scores, keys), mask)
+            outs[frame, :, cols] = part + jnp.where(joined, outs[before, :, cols], 0.0)
+        grad_kv = jnp.concatenate(key_parts + value_parts, axis=1).astype(BF16)
+        hat, scale = normalise(m_ref[...].astype(F32))
+        gain = gb_ref[0:1, :]
+        normed = (hat * gain + gb_ref[3:4, :]).astype(BF16)
+        weight_acc[...] += mm_tn(normed, grad_kv)
+        grad = mm_nt(grad_kv, w_ref[:, inner : 3 * inner])
+        gain_acc[0:1, :] += jnp.sum(grad * hat, axis=0, keepdims=True)
+        gain_acc[1:2, :] += jnp.sum(grad, axis=0, keepdims=True)
+        media_grad[...] = norm_back(grad, hat, scale, gain).astype(BF16)
+
+    @pl.when(step == frames + 1)
+    def _():
+        wide = latent_mask(rows, inner)
+
+        @pl.loop(0, clips)
+        def _(clip):
+            out, grad_kv = latent_attention_back(
+                clip_queries(clip),
+                clip_grads(clip),
+                clip_stats(clip),
+                kl_ref[clip],
+                vl_ref[clip],
+                wide,
+            )
+            latent_kv[clip] = grad_kv
+            out = (out + jnp.where(has[clip] == 1, outs[last[clip]], 0.0)) * SCALE
+            for r in range(4):
+                part = slice(r * rows, (r + 1) * rows)
+                if r % 2:
+                    send[r // 2, clip] = out[part].astype(BF16)
+                else:
+                    keep[r // 2, clip] = out[part]
+
+        core_copy.start()
+        hat, scale = normalise(lat_ref[...])
+        gain = gb_ref[1:2, :]
+        normed = (hat * gain + gb_ref[4:5, :]).astype(BF16)
+        core_copy.wait()
+        away[...] = (keep[1] + core_q[1].astype(F32)).astype(BF16)
+        y_copy.start()
+        grad_kv = latent_kv[...].reshape(total_rows, 2 * inner)
+        pack_ref[:, inner : 3 * inner] = (weight_acc[...] + mm_tn(normed, grad_kv)).astype(BF16)
+        grad = mm_nt(grad_kv, w_ref[:, inner : 3 * inner])
+        mixed = weight_acc.at[:total_rows]
+        load_mixed = pltpu.make_async_copy(mixed_ref, mixed, mixed_sem)
+        load_mixed.start()
+        scatter.run(plan[-1][1])
+        y_copy.wait()
+        grad_q = (keep[0] + core_q[0].astype(F32) + y_q[...].astype(F32)).astype(BF16)
+        grad_q = grad_q.reshape(total_rows, inner)
+        grad = grad + mm_nt(grad_q, w_ref[:, :inner])
+        pack_ref[:, :inner] = mm_tn(normed, grad_q).astype(BF16)
+        table = jnp.concatenate(
+            [
+                gain_acc[0:1, :],
+                jnp.sum(grad * hat, axis=0, keepdims=True),
+                gain_f[0:1, :],
+                gain_acc[1:2, :],
+                jnp.sum(grad, axis=0, keepdims=True),
+                gain_f[1:2, :],
+                jnp.zeros((LANES - 6, grad.shape[1]), F32),
+            ],
+            axis=0,
+        )
+        pack_ref[:, 3 * inner :] = table.T.astype(BF16)
+        load_mixed.wait()
+        latents_grad[...] = mixed[...] + norm_back(grad, hat, scale, gain)
+        scatter.finish(mine_ref)
+
+
+def back(
+    ids,
+    last,
+    has,
+    same,
+    grad_feed,
+    query_all,
+    context_grad,
+    tile,
+    keys,
+    values,
+    media,
+    latent_key,
+    latent_value,
+    gains,
+    attend,
+    latents,
+    mixed_grad,
+    gain_f,
+    depth,
+    chunk,
+    plan,
+):
+    clips, rows, inner = latent_key.shape
+    frames = media.shape[0] // PATCH_IMG
+    width = media.shape[1]
+    total = clips * rows
+    cut = (clips, rows, inner)
+    _, feed_rows, feed_cols = grad_feed.shape
+    once = pl.Buffered(buffer_count=1)
+
+    def whole(x):
+        return pl.BlockSpec(x.shape, lambda i: (0,) * len(x.shape), pipeline_mode=once)
+
+    def block(columns):
+        return pl.BlockSpec((PATCH_IMG, columns), lambda i: (jnp.clip(i - 1, 0, frames - 1), 0))
+
+    smem = pl.BlockSpec(memory_space=pltpu.SMEM)
+    outs = (
+        jax.ShapeDtypeStruct(media.shape, BF16),
+        jax.ShapeDtypeStruct(latents.shape, F32),
+        jax.ShapeDtypeStruct(attend.shape, BF16),
+        jax.ShapeDtypeStruct((feed_rows, feed_cols), F32),
+    )
+    return pl.pallas_call(
+        functools.partial(back_kernel, depth, frames, chunk, plan),
+        grid=(frames + 2,),
+        out_shape=outs,
+        in_specs=[smem] * 4
+        + [any_spec(), whole(query_all), whole(context_grad), whole(tile)]
+        + [block(inner), block(inner), block(width)]
+        + [whole(x) for x in (latent_key, latent_value, gains, attend, latents)]
+        + [any_spec(), whole(gain_f)],
+        out_specs=(block(width),) + tuple(whole(x) for x in outs[1:]),
+        scratch_shapes=scatter_buffers(depth, feed_rows, feed_cols)
+        + scatter_sems(depth)
+        + [
+            pltpu.VMEM((4,) + cut, BF16),
+            pltpu.VMEM((4, 2 * HEADS, total), F32),
+            pltpu.VMEM((4, clips, rows, LANES), F32),
+            pltpu.VMEM((width, 2 * inner), F32),
+            pltpu.VMEM((8, width), F32),
+            pltpu.VMEM((frames, 4 * rows, inner), F32),
+            pltpu.VMEM((clips, rows, 2 * inner), BF16),
+            pltpu.VMEM((2,) + cut, F32),
+            pltpu.VMEM((2,) + cut, BF16),
+            pltpu.VMEM((2,) + cut, BF16),
+            pltpu.VMEM(cut, BF16),
+            pltpu.VMEM(cut, BF16),
+            pltpu.SemaphoreType.DMA((8,)),
+            pltpu.SemaphoreType.DMA((8,)),
+            pltpu.SemaphoreType.DMA,
+        ],
+        compiler_params=params(collective_id=4, has_side_effects=True),
+        name="back",
+    )(
+        ids,
+        last,
+        has,
+        same,
+        grad_feed,
+        query_all,
+        context_grad,
+        tile,
+        keys,
+        values,
+        media,
+        latent_key,
+        latent_value,
+        gains,
+        attend,
+        latents,
+        mixed_grad,
+        gain_f,
+    )
+
+
 def pack_feed(expand, shrink, output):
     width = shrink.shape[-1]
     groups = expand.shape[-1] // width
@@ -1101,8 +2000,6 @@
             expand_weight.astype(BF16), shrink_weight.astype(BF16), output_weight.astype(BF16)
         )
         attend = gather_fast(attend_shard, depth, 1).reshape(width, attend_shard.shape[1])
-        attend, feed_shard = lax.optimization_barrier((attend, feed_shard))
-        feed = gather_fast(feed_shard, depth, 2)
     else:
 
         def everywhere(x):
@@ -1123,69 +2020,116 @@
     ids = jnp.clip(ids, 0, samples - 1)
 
     latent_flat = latents.reshape(rows, width)
-    query, latent_key, latent_value = latent_project(latent_flat, gains, attend, inner)
     cut = (samples, lat_dev, inner)
-    latent_key = latent_key.reshape(cut)
-    latent_value = latent_value.reshape(cut)
 
     def to_group(own):
         other = over_y(own)
         return [own, over_core(own), other, over_core(other)]
 
-    queries = to_group(query.reshape(cut))
-    keys, values = media_project(media, gains, attend, inner)
-    keep, send, keep_st, send_st = attention_forward(
-        ids, queries, keys, values, latent_key, latent_value
-    )
-    got, got_st = over_core(send), over_core(send_st)
-    flat_o, flat_s = (2, rows, inner), (2, rows, LANES)
-    own, own_st, away, away_st = join_cores(
-        keep.reshape(flat_o), keep_st.reshape(flat_s), got.reshape(flat_o), got_st.reshape(flat_s)
-    )
-    got, got_st = over_y(away), over_y(away_st)
+    if fast:
+        clip = jnp.arange(samples, dtype=jnp.int32)
+        here = ids[None, :] == clip[:, None]
+        has = jnp.any(here, axis=1).astype(jnp.int32)
+        last = jnp.max(jnp.where(here, jnp.arange(frames, dtype=jnp.int32)[None, :], 0), axis=1)
+        same = jnp.concatenate([jnp.zeros((1,), jnp.int32), (ids[1:] == ids[:-1]).astype(jnp.int32)])
+        feed, keys, values, query_all, latent_key, latent_value, own, own_st, got, got_st = front(
+            ids,
+            last,
+            has,
+            same,
+            feed_shard,
+            media,
+            latent_flat,
+            gains,
+            attend,
+            samples,
+            inner,
+            depth,
+            FRONT_PLAN,
+        )
+    else:
+        query, latent_key, latent_value = latent_project(latent_flat, gains, attend, inner)
+        latent_key = latent_key.reshape(cut)
+        latent_value = latent_value.reshape(cut)
+        queries = to_group(query.reshape(cut))
+        keys, values = media_project(media, gains, attend, inner)
+        keep, send, keep_st, send_st = attention_forward(
+            ids, queries, keys, values, latent_key, latent_value
+        )
+        got, got_st = over_core(send), over_core(send_st)
+        flat_o, flat_s = (2, rows, inner), (2, rows, LANES)
+        own, own_st, away, away_st = join_cores(
+            keep.reshape(flat_o),
+            keep_st.reshape(flat_s),
+            got.reshape(flat_o),
+            got_st.reshape(flat_s),
+        )
+        got, got_st = over_y(away), over_y(away_st)
     cot_flat = cotangent.reshape(rows, width)
     out_rows, mixed_grad, context_grad, tile, gain_f, grad_feed = feed_forward(
         own, own_st, got, got_st, latent_flat, cot_flat, gains, feed
     )
-    grads = to_group(context_grad.reshape(cut))
-    tiles = to_group(tile.reshape(samples, lat_dev, LANES))
-    grad_media, latent_kv, keep, send, grad_kv, gain_m = attention_backward(
-        ids,
-        queries,
-        grads,
-        tiles,
-        keys,
-        values,
-        latent_key,
-        latent_value,
-        media,
-        gains,
-        attend,
-    )
-    got = over_core(send)
-    pair = keep.astype(F32) + got.astype(F32)
-    got = over_y(pair[1].astype(BF16))
-    latents_grad, grad_attend = latent_backward(
-        latent_flat,
-        mixed_grad,
-        pair[0].reshape(rows, inner),
-        got.reshape(rows, inner),
-        latent_kv.reshape(rows, 2 * inner),
-        gains,
-        attend,
-        grad_kv,
-        gain_m,
-        gain_f,
-    )
     if fast:
+        grad_media, latents_grad, grad_attend, mine_feed = back(
+            ids,
+            last,
+            has,
+            same,
+            grad_feed,
+            query_all,
+            context_grad.reshape(cut),
+            tile,
+            keys,
+            values,
+            media,
+            latent_key,
+            latent_value,
+            gains,
+            attend,
+            latent_flat,
+            mixed_grad,
+            gain_f,
+            depth,
+            16,
+            BACK_PLAN,
+        )
         mine = scatter_fast(
             grad_attend.reshape(BLOCKS, attend_rows, grad_attend.shape[1]), depth, 3, 16
         )
-        mine_feed = scatter_fast(grad_feed, depth, 4, 16)
         own_expand, own_shrink, own_output = unpack_feed(
             mine_feed, attend_rows, shrink_weight.shape[0]
         )
     else:
+        grads = to_group(context_grad.reshape(cut))
+        tiles = to_group(tile.reshape(samples, lat_dev, LANES))
+        grad_media, latent_kv, keep, send, grad_kv, gain_m = attention_backward(
+            ids,
+            queries,
+            grads,
+            tiles,
+            keys,
+            values,
+            latent_key,
+            latent_value,
+            media,
+            gains,
+            attend,
+        )
+        got = over_core(send)
+        pair = keep.astype(F32) + got.astype(F32)
+        got = over_y(pair[1].astype(BF16))
+        latents_grad, grad_attend = latent_backward(
+            latent_flat,
+            mixed_grad,
+            pair[0].reshape(rows, inner),
+            got.reshape(rows, inner),
+            latent_kv.reshape(rows, 2 * inner),
+            gains,
+            attend,
+            grad_kv,
+            gain_m,
+            gain_f,
+        )
 
         def owners(x):
             return lax.psum_scatter(x.astype(F32), AXES, scatter_dimension=0, tiled=True)

time: 490 us -> 371 us (0.76)
  Pallas kernels: 416 us -> 327 us
  waiting for transfers between devices: 18 us -> 0 us
  starting transfers between devices: 8.3 us -> 0 us
  local copies, waits for them, and re-layouts: 16.7 us -> 11.4 us
    pallas_call x2 -> x1, Pallas kernels: 134 us -> 31.6 us  [scatter_fast(): pl.pallas_call(functools.partial(scatter_kernel, depth, chunk), out_shape...]
    pallas_call x6 -> x2, Pallas kernels: 123 us -> 225 us  [the longest x1 113 us: front(): pl.pallas_call(functools.partial(front_kernel, depth, frames, plan), grid...]
    pallas_call x2 -> x1, Pallas kernels: 116 us -> 27.6 us  [gather_fast(): pl.pallas_call(functools.partial(gather_kernel, depth), out_shape=jax.Sha...]
    ppermute x15 -> x0, waiting for transfers between devices: 18 us -> none  [the longest x3 13.1 us: to_group(): other = over_y(own)]
    ppermute x15 -> x0, starting transfers between devices: 8.3 us -> none  [the longest x3 3.05 us: to_group(): other = over_y(own)]
    unnamed x84 -> x56, local copies, waits for them, and re-layouts: 9.89 us -> 8.05 us
  transfers between devices with their start and end apart: 15 -> 0, of which waited for: 6 -> 0; matrix products, arithmetic and copies ran while one was open for 2% -> 0% of each run, Pallas kernels for 43% -> 0%
where the time goes in v2:
time: 371 us; the launch traced here: 364 us
  Pallas kernels  327 us (88%)
  other arithmetic  18.9 us (5%)
  local copies, waits for them, and re-layouts  11.4 us (3%)
  between operations  7.18 us (2%)
    pallas_call x1, Pallas kernels, front(): pl.pallas_call(functools.partial(front_kernel, depth, frames, plan), grid...  113 us
    pallas_call x1, Pallas kernels, back(): pl.pallas_call(functools.partial(back_kernel, depth, frames, chunk, plan)...  111 us
    pallas_call x1, Pallas kernels, feed_forward(): pl.pallas_call(feed_kernel, out_shape=(jax.ShapeDtypeStruct((rows, width)...  33.6 us
    pallas_call x1, Pallas kernels, scatter_fast(): pl.pallas_call(functools.partial(scatter_kernel, depth, chunk), out_shape...  31.6 us
    pallas_call x1, Pallas kernels, gather_fast(): pl.pallas_call(functools.partial(gather_kernel, depth), out_shape=jax.Sha...  27.6 us
    pallas_call x1, Pallas kernels, total_fast(): pl.pallas_call(functools.partial(total_kernel, images, lats), out_shape=j...  9.5 us
    unnamed x56, local copies, waits for them, and re-layouts  8.05 us
    add x5, other arithmetic, shards(): new_smoothed.append(AVERAGING * average + (1.0 - AVERAGING) * master_new)  7.77 us

profile of v2, /device:TPU:0, one launch (start us, length us, event | category | flops | bytes accessed | tf_op | source)
XLA Modules:
  0.0 364.3 jit_solution(13704484336018694149)
XLA Ops:
  0.7 0.8 broadcast_multiply_fusion.4
  1.5 0.9 convert.15
  2.5 0.7 fusion.1.x_ref
  3.1 27.6 %gather1.1 = bf16[32,32,1664]{2,1,0:T(8,128)(2,1)} custom-call(bf16[32,1664]{1,0:T(8,128)(2,1)} %fusion.1.x_ref), custom_call_target="tpu_custom_call" | custom-call | tf_op jit(solution)/shard_map/gather1/pallas_call | solution.py:201
  30.8 1.1 convert_bitcast_fusion
  31.8 0.8 copy.157.gb_ref
  35.1 0.8 pad_maximum_fusion.shard_ref
  35.9 113.2 %front.1 = (bf16[32,272,1024]{2,1,0:T(8,128)(2,1)}, bf16[3072,512]{1,0:T(8,128)(2,1)}, bf16[3072,512]{1,0:T(8,128)(2,1)}, bf16[4,24,16,512]{3,2,1,0:T(8,128)(2,1...) custom-call(s32[12]{0:T(128)} %copy-done.15, ...), custom_call_target="tpu_custom_call" | custom-call | tf_op jit(solution)/shard_map/front/pallas_call | solution.py:1003
  149.1 33.6 %feed_forward.1 = (f32[384,1024]{1,0:T(8,128)}, f32[384,1024]{1,0:T(8,128)}, bf16[384,512]{1,0:T(8,128)(2,1)}, f32[384,128]{1,0:T(8,128)}, f32[8,1024]{1,0:T(8,128)}, /*index=5*/bf16[32,272,1024]{2,1,0:T(8,128)(2,1)}) custom-call(f32[384,512]{1,0:T(8,128)} %get-tuple-element.42.own, f32[384,128]{1,0:T(8,128)} %get-tuple-element.43.own_st, ...), custom_call_target="tpu_custom_call" | custom-call | flops 20535312384 | bytes 35651584 | tf_op jit(solution)/shard_map/feed_forward/pallas_call | solution.py:1224
  182.7 111.4 %back.1 = (bf16[3072,1024]{1,0:T(8,128)(2,1)}, f32[384,1024]{1,0:T(8,128)}, bf16[1024,1664]{1,0:T(8,128)(2,1)}, f32[272,1024]{1,0:T(8,128)}) custom-call(s32[12]{0:T(128)} %copy-done.15, s32[24]{0:T(128)} %select_reduce_fusion.last, s32[24]{0:T(128)} %convert_element_type.21.has, s32[12]{0:T(128)} %add_convert_fusion.same, ...), custom_call_target="tpu_custom_call" | custom-call | tf_op jit(solution)/shard_map/back/pallas_call | solution.py:1867
  294.2 31.6 %scatter3.1 = f32[32,1664]{1,0:T(8,128)} custom-call(bf16[32,32,1664]{2,1,0:T(8,128)(2,1)} %bitcast.31), custom_call_target="tpu_custom_call" | custom-call | tf_op jit(solution)/shard_map/scatter3/pallas_call | solution.py:323
  325.8 1.7 multiply_reduce_fusion.2
  329.4 0.7 multiply_reduce_fusion
  331.5 1.5 multiply_reduce_fusion.4
  334.8 9.5 %total5.1 = f32[8,128]{1,0:T(8,128)} custom-call(f32[8,128]{1,0:T(8,128)} %broadcast_in_dim.22.x_ref), custom_call_target="tpu_custom_call" | custom-call | tf_op jit(solution)/shard_map/total5/pallas_call | solution.py:385
  344.3 1.2 slice.42
  347.0 0.9 multiply_add_fusion.12
  347.9 0.7 copy.173
  351.8 2.9 multiply_add_fusion
  354.8 2.5 multiply_add_fusion.1
  357.3 0.7 multiply_add_fusion.9
  358.0 0.9 multiply_add_fusion.6
  358.9 2.7 copy.185
  361.6 1.1 copy.186
  (84 shorter events, 7.9 us)
Async XLA Ops:
  3.1 29.5 %copy-start.20 = (s32[1,24]{1,0:T(1,128)S(1)}, s32[1,24]{1,0:T(1,128)}, u32[]{:S(2)}) copy-start(s32[1,24]{1,0:T(1,128)} %param.24) | copy-start | bytes 292
  30.7 4.2 %copy-start.3 = (f32[32,4096]{1,0:T(8,128)S(1)}, f32[32,4096]{1,0:T(8,128)}, u32[]{:S(2)}) copy-start(f32[32,4096]{1,0:T(8,128)} %param.28) | copy-start | bytes 1572868
  30.7 4.3 %copy-start.2 = (f32[128,1024]{1,0:T(8,128)S(1)}, f32[128,1024]{1,0:T(8,128)}, u32[]{:S(2)}) copy-start(f32[128,1024]{1,0:T(8,128)} %param.29) | copy-start | bytes 1572868
  30.7 4.3 %copy-start.8 = (f32[16,1024]{1,0:T(8,128)S(1)}, f32[16,1024]{1,0:T(8,128)}, u32[]{:S(2)}) copy-start(f32[16,1024]{1,0:T(8,128)} %param.27) | copy-start | bytes 196612
  33.1 2.9 copy-start.15
  294.1 33.4 %copy-start = (f32[272,1024]{1,0:T(8,128)S(1)}, f32[272,1024]{1,0:T(8,128)}, u32[]{:S(2)}) copy-start(f32[272,1024]{1,0:T(8,128)} %get-tuple-element.61) | copy-start | bytes 3342340
  294.1 52.3 %copy-start.16 = (f32[32,3]{0,1:T(4,128)S(1)}, f32[32,3]{0,1:T(4,128)}, u32[]{:S(2)}) copy-start(f32[32,3]{0,1:T(4,128)} %param.36) | copy-start | bytes 1156
  294.1 52.4 %copy-start.17 = (f32[32,3]{0,1:T(4,128)S(1)}, f32[32,3]{0,1:T(4,128)}, u32[]{:S(2)}) copy-start(f32[32,3]{0,1:T(4,128)} %param.37) | copy-start | bytes 1156
  294.1 52.5 %copy-start.18 = (f32[32,3]{0,1:T(4,128)S(1)}, f32[32,3]{0,1:T(4,128)}, u32[]{:S(2)}) copy-start(f32[32,3]{0,1:T(4,128)} %param.42) | copy-start | bytes 1156
  294.1 52.6 %copy-start.19 = (f32[32,3]{0,1:T(4,128)S(1)}, f32[32,3]{0,1:T(4,128)}, u32[]{:S(2)}) copy-start(f32[32,3]{0,1:T(4,128)} %param.43) | copy-start | bytes 1156
  294.1 52.7 %copy-start.13 = (f32[32,3]{0,1:T(4,128)S(1)}, f32[32,3]{0,1:T(4,128)}, u32[]{:S(2)}) copy-start(f32[32,3]{0,1:T(4,128)} %param.30) | copy-start | bytes 1156
  294.2 52.8 %copy-start.14 = (f32[32,3]{0,1:T(4,128)S(1)}, f32[32,3]{0,1:T(4,128)}, u32[]{:S(2)}) copy-start(f32[32,3]{0,1:T(4,128)} %param.31) | copy-start | bytes 1156
  325.8 33.1 %slice-start = ((s8[6291456]{0:T(1024)(128)(4,1)}), s8[2097152]{0:T(1024)(128)(4,1)S(1)}, s32[]{:S(2)}) async-start(s8[6291456]{0:T(1024)(128)(4,1)} %bitcast.29), calls=%async_computation | async-start | bytes 4194304
  351.8 2.9 copy-start.4
  351.8 2.9 copy-start.7
  351.8 7.1 %slice-start.1 = ((s8[6291456]{0:T(1024)(128)(4,1)}), s8[4194304]{0:T(1024)(128)(4,1)S(1)}, s32[]{:S(2)}) async-start(s8[6291456]{0:T(1024)(128)(4,1)} %bitcast.29), calls=%async_computation.1 | async-start | bytes 8388608
  354.7 2.5 copy-start.11
  354.7 2.5 copy-start.12
  354.8 3.2 copy-start.1
  354.8 3.2 copy-start.6
  354.8 3.2 copy-start.9
  354.8 3.2 copy-start.10
  358.9 2.7 copy-start.5
